TPU v7x, 512 devices: a whole 4x4x16 slice. The times are simulated.
512 devices in a mesh: sample: 16 (over z_lo, core), ctx: 32 (over x, z_hi, y).
Axes of the slice: x: 4, y: 4, z: 16 (z_hi: 2, z_lo: 8; z = z_hi * 8 + z_lo), core: 2. Of those that a mesh axis runs over, the one named last changes fastest.
Arguments:
- queries: bfloat16 [65536, 2048], P(('sample', 'ctx')), may hold values from -4 to 4
- experts: int32 [65536, 16], P(('sample', 'ctx')), may hold values from 0 to 63, all different within a row; in each aligned block of 128 rows (0 to 127, 128 to 255, ...) at most 64 rows name the same one
- gate: float32 [65536, 16], P(('sample', 'ctx')), may hold values from 0.05 to 1
- prefix_keys: bfloat16 [512, 1024], P('ctx'), may hold values from -8 to 8
- prefix_values: bfloat16 [512, 1024], P('ctx'), may hold values from -6 to 6
- d_out: bfloat16 [65536, 2048], P(('sample', 'ctx')), may hold values from -6 to 6
- lengths: int32 [64], replicated, may hold values from 128 to 1024
Outputs:
- attended: bfloat16 [65536, 2048], P(('sample', 'ctx'))
- query_grad: bfloat16 [65536, 2048], P(('sample', 'ctx'))
- gate_grad: float32 [65536, 16], P(('sample', 'ctx'))
- key_grad: float32 [512, 1024], P('ctx')
- value_grad: float32 [512, 1024], P('ctx')
Inputs may be any that keep to these rules, and one draw needn't show every extreme that they name: `experts`: among the tokens of one device (aligned blocks of 128 tokens) no expert is picked more than 64 times, and some expert is picked exactly 64 times; a token's picks are distinct. Completion c holds tokens c * 1024 to (c + 1) * 1024 - 1; its first lengths[c] tokens are live.
All inputs are finite; a program needn't handle non-finite values.
Results may differ from a plain program's by a relative error of at most 0.012.
Values may be sent and summed in bfloat16 or wider, within the bound.
A program may use at most 64 MiB of HBM per device.

v0:
```python
import jax
import jax.numpy as jnp
from jax import lax
from jax.sharding import Mesh
from jax.sharding import PartitionSpec as P

HEAD = 128
KV_HEADS = 8
EXPERTS = 64
TOPK = 16
CLEN = 1024
CAP = 64
CTX = ("ctx_0", "ctx_1", "ctx_2")
SAMPLE_CTX = ("sample", "ctx_0", "ctx_1", "ctx_2")


def side_by_side(arrays, axis, dim, along):
    ends, at = ([], 0)
    for a in arrays[:-1]:
        at += a.shape[along]
        ends.append(at)
    both = jnp.concatenate(arrays, axis=along)
    return tuple(jnp.split(lax.all_gather(both, axis, axis=dim, tiled=True), ends, axis=along))


def reduced_to_own(pieces, axes, turns):
    lengths = [lax.axis_size(a) for a in axes]
    pieces = pieces.reshape(*lengths, *pieces.shape[1:])
    pieces = pieces.transpose(*turns, *range(len(axes), pieces.ndim))
    pieces = pieces.reshape(-1, *pieces.shape[len(axes) :])
    for k in turns:
        pieces = lax.psum_scatter(pieces, axes[k], scatter_dimension=0, tiled=True)
    return pieces[0]


def split_up(shard, dim, size):
    before, after = (shard.shape[:dim], shard.shape[dim + 1 :])
    return jnp.moveaxis(shard.reshape(*before, size, -1, *after), dim, 0)


def summed_rows(shard, axes, turns, dim):
    size = lax.axis_size(axes)
    return reduced_to_own(split_up(shard, dim, size), axes, turns)


def sent_to_all(shard, axis):
    size = lax.axis_size(axis)
    return lax.all_to_all(
        jnp.broadcast_to(shard[None], (size, *shard.shape)), axis, 0, 0, tiled=True
    )


def over_copies(shard, axis):
    everything = sent_to_all(shard, axis)
    return jnp.sum(everything, axis=0)


def slot_index(experts):
    flat = experts.reshape(-1)
    picked = (flat[:, None] == jnp.arange(EXPERTS, dtype=jnp.int32)[None, :]).astype(jnp.int32)
    before = jnp.cumsum(picked, axis=0) - picked
    return flat * CAP + jnp.sum(before * picked, axis=1)


def over_blocks(step, carry, pieces, start):
    keys, values = pieces
    length = keys.shape[0]

    def inner(state, number):
        begin = number * 128
        key_block = lax.dynamic_slice_in_dim(keys, begin, 128, 0)
        value_block = lax.dynamic_slice_in_dim(values, begin, 128, 0)
        return (step(state, key_block, value_block, start + begin), None)

    carry, _ = lax.scan(inner, carry, jnp.arange(length // 128, dtype=jnp.int32))
    return carry


def local(queries, experts, gate, prefix_keys, prefix_values, d_out, lengths):
    scale = HEAD ** (-0.5)
    width = KV_HEADS * HEAD
    group = EXPERTS * CAP // KV_HEADS
    rows = queries.shape[0]
    n_ctx = lax.axis_size(CTX)
    prefix_total = prefix_keys.shape[0] * n_ctx
    block = lax.axis_index("sample") * n_ctx + lax.axis_index(CTX)
    token_ids = block * rows + jnp.arange(rows, dtype=jnp.int32)
    owners = (token_ids // CLEN)[:, None] == jnp.arange(lengths.shape[0], dtype=jnp.int32)[None, :]
    chosen = jnp.sum(jnp.where(owners, lengths[None, :], 0), axis=1)
    live = (token_ids % CLEN < chosen).astype(jnp.float32)
    slots = slot_index(experts)
    q_buf = jnp.zeros((EXPERTS * CAP, HEAD), jnp.bfloat16).at[slots].set(queries.reshape(-1, HEAD))
    q_buf = q_buf.reshape(KV_HEADS, group, HEAD)

    def scores_of(key_block):
        heads = key_block.reshape(-1, KV_HEADS, HEAD)
        return jnp.einsum("hgd,phd->hgp", q_buf, heads, preferred_element_type=jnp.float32) * scale

    def forward_step(carry, key_block, value_block, start):
        high, total, accum = carry
        score = scores_of(key_block)
        new_high = jnp.maximum(high, jnp.max(score, axis=2))
        shrink = jnp.exp(high - new_high)
        weight = jnp.exp(score - new_high[..., None])
        total = total * shrink + jnp.sum(weight, axis=2)
        heads = value_block.reshape(-1, KV_HEADS, HEAD)
        accum = accum * shrink[..., None] + jnp.einsum(
            "hgp,phd->hgd", weight.astype(jnp.bfloat16), heads, preferred_element_type=jnp.float32
        )
        return (new_high, total, accum)

    start_state = (
        jnp.full((KV_HEADS, group), -1e30, jnp.float32),
        jnp.zeros((KV_HEADS, group), jnp.float32),
        jnp.zeros((KV_HEADS, group, HEAD), jnp.float32),
    )
    gathered = side_by_side((prefix_keys, prefix_values), CTX, 0, 1)
    high, total, accum = over_blocks(forward_step, start_state, gathered, 0)
    output = accum / total[..., None]
    lse = high + jnp.log(total)
    o_rows = output.reshape(EXPERTS * CAP, HEAD)[slots].reshape(rows, TOPK, HEAD)
    cot = d_out.astype(jnp.float32).reshape(rows, TOPK, HEAD)
    factor = gate * live[:, None]
    attended = (factor[..., None] * o_rows).reshape(rows, TOPK * HEAD).astype(jnp.bfloat16)
    gate_grad = live[:, None] * jnp.sum(o_rows * cot, axis=2)
    dout_rows = (factor[..., None] * cot).astype(jnp.bfloat16)
    dout_buf = (
        jnp.zeros((EXPERTS * CAP, HEAD), jnp.bfloat16).at[slots].set(dout_rows.reshape(-1, HEAD))
    )
    dout_buf = dout_buf.reshape(KV_HEADS, group, HEAD)
    delta = jnp.sum(dout_buf.astype(jnp.float32) * output, axis=2)

    def backward_step(carry, key_block, value_block, start):
        dq_accum, grads = carry
        key_heads = key_block.reshape(-1, KV_HEADS, HEAD)
        value_heads = value_block.reshape(-1, KV_HEADS, HEAD)
        prob = jnp.exp(scores_of(key_block) - lse[..., None])
        dprob = jnp.einsum(
            "hgd,phd->hgp", dout_buf, value_heads, preferred_element_type=jnp.float32
        )
        dscore = (prob * (dprob - delta[..., None])).astype(jnp.bfloat16)
        dq_accum = (
            dq_accum
            + jnp.einsum("hgp,phd->hgd", dscore, key_heads, preferred_element_type=jnp.float32)
            * scale
        )
        key_part = (
            jnp.einsum("hgp,hgd->phd", dscore, q_buf, preferred_element_type=jnp.float32) * scale
        )
        value_part = jnp.einsum(
            "hgp,hgd->phd", prob.astype(jnp.bfloat16), dout_buf, preferred_element_type=jnp.float32
        )
        joined = jnp.concatenate(
            [key_part.reshape(-1, width), value_part.reshape(-1, width)], axis=1
        )
        grads = lax.dynamic_update_slice_in_dim(grads, joined, start, 0)
        return (dq_accum, grads)

    back_state = (
        jnp.zeros((KV_HEADS, group, HEAD), jnp.float32),
        jnp.zeros((prefix_total, 2 * width), jnp.float32),
    )
    dq_buf, grads = over_blocks(backward_step, back_state, gathered, 0)
    query_grad = (
        dq_buf.reshape(EXPERTS * CAP, HEAD)[slots].reshape(rows, TOPK * HEAD).astype(jnp.bfloat16)
    )
    share = summed_rows(grads, CTX, (0, 2, 1), 0)
    summed = over_copies(share, "sample")
    return (attended, query_grad, gate_grad, summed[:, :width], summed[:, width:])


def solution(mesh):
    torus = Mesh(
        mesh.devices.reshape(mesh.shape["sample"], 4, 2, 4), ("sample", "ctx_0", "ctx_1", "ctx_2")
    )
    in_specs = (
        P(SAMPLE_CTX, None),
        P(SAMPLE_CTX, None),
        P(SAMPLE_CTX, None),
        P(CTX, None),
        P(CTX, None),
        P(SAMPLE_CTX, None),
        P(),
    )
    out_specs = (
        P(SAMPLE_CTX, None),
        P(SAMPLE_CTX, None),
        P(SAMPLE_CTX, None),
        P(CTX, None),
        P(CTX, None),
    )
    return jax.shard_map(local, mesh=torus, in_specs=in_specs, out_specs=out_specs, check_vma=False)
```

profile of v0, /device:TPU:117, one launch (start us, length us, event | category | flops | bytes accessed | tf_op | source)
XLA Modules:
  0.0 472.4 jit_solution(16044423474720644806)
XLA Ops:
  7.2 1.5 pad_maximum_fusion.1
  8.8 0.8 copy.77
  9.8 0.7 broadcast_multiply_fusion.2
  10.7 0.8 copy.75
  11.5 0.7 select_reduce_fusion
  12.5 18.1 %reduce-window.6 = s32[64,16,128]{2,1,0:T(8,128)S(1)} reduce-window(s32[64,16,128]{2,1,0:T(8,128)S(1)} %fusion.24, s32[]{:T(128)} %constant.93.clone.1), window={size=1x1x128 pad=0_0x0_0x127_0}, to_apply=%region_1.2 | reduce-window | flops 16646144 | bytes 1048580 | tf_op jit(solution)/shard_map/reduce-window
  31.4 1.0 reshape.191
  33.2 6.4 %scatter_custom_fusion = bf16[4096,128]{1,0:T(8,128)(2,1)S(1)} fusion(s32[2048]{0:T(1024)S(1)} %bitcast.139, bf16[2048,128]{1,0:T(8,128)(2,1)} %reshape.191, bf16[]{:T(256)} %constant.101.clone.1), kind=kCustom, calls=%fused_computation.48 | custom fusion | bytes 1049088 | tf_op jit(solution)/shard_map/scatter | solution.py:92
  39.6 7.2 %scatter_custom_fusion.1 = bf16[4096,128]{1,0:T(8,128)(2,1)S(1)} fusion(s32[2048]{0:T(1024)S(1)} %bitcast.140, f32[2048,128]{1,0:T(8,128)S(1)} %reshape.170, f32[2048]{0:T(1024)S(1)} %mul.135, bf16[]{:T(256)} %constant.101.clone.1), kind=kCustom, calls=%fused_computation.39 | custom fusion | flops 524288 | bytes 2105346 | tf_op jit(solution)/shard_map/scatter | solution.py:128
  48.4 87.0 %all-gather.2.cloned.1.call-done = bf16[512,2048]{1,0:T(8,128)(2,1)} async-done(((bf16[16,2048]{1,0:T(8,128)(2,1)}), bf16[512,2048]{1,0:T(8,128)(2,1)}) %all-gather.2.cloned.1.call-update) | async-done | bytes 2097168 | tf_op jit(solution)/shard_map/all_gather | solution.py:23
  135.4 3.0 fusion.25
  138.4 2.3 copy.82
  140.7 2.3 copy.81
  143.0 26.4 %while.28 = (s32[]{:T(128)}, f32[8,512]{1,0:T(8,128)S(1)}, f32[8,512]{1,0:T(8,128)S(1)}, f32[8,512,128]{2,1,0:T(8,128)}, s32[4]{0:T(128)S(1)}, /*index=5*/bf16[5...) while((s32[]{:T(128)}, f32[8,512]{1,0:T(8,128)S(1)}, ...), condition=%wide.region_8.9_spmd.clone, body=%wide.region_5.8_spmd.clone.sunk | while | flops 274223104 | bytes 30146816 | solution.py:75
  144.3 1.1 constant_dynamic-slice_fusion.6
  146.9 1.3 fusion.65
  148.3 1.3 copy-done.3
  150.9 1.1 constant_dynamic-slice_fusion.6
  153.5 1.3 fusion.65
  154.9 1.3 copy-done.3
  157.4 1.1 constant_dynamic-slice_fusion.6
  160.1 1.3 fusion.65
  161.5 1.3 copy-done.3
  164.0 1.1 constant_dynamic-slice_fusion.6
  166.7 1.3 fusion.65
  168.1 1.3 copy-done.3
  169.4 3.7 multiply_reduce_fusion
  173.1 2.4 broadcast_in_dim.28.clone
  175.6 49.1 %while.29 = (s32[]{:T(128)}, f32[8,512,128]{2,1,0:T(8,128)}, f32[512,2048]{1,0:T(8,128)}, s32[4]{0:T(128)S(1)}, bf16[512,1024]{0,1:T(8,128)(2,1)}, /*index=5*/bf...) while((s32[]{:T(128)}, f32[8,512,128]{2,1,0:T(8,128)}, ...), condition=%wide.region_12.13_spmd.clone, body=%wide.region_11.12_spmd.clone.sunk | while | flops 677249024 | bytes 31244532 | solution.py:75
  176.8 1.1 constant_dynamic-slice_fusion.7
  180.1 1.0 pad_maximum_fusion.3
  181.1 2.6 copy.110
  183.7 1.8 select_add_fusion.2
  185.5 1.1 constant_dynamic-update-slice_fusion.2
  187.8 1.1 constant_dynamic-slice_fusion.7
  191.1 1.0 pad_maximum_fusion.3
  192.1 2.6 copy.110
  194.7 3.5 select_add_fusion.2
  198.2 1.1 constant_dynamic-update-slice_fusion.2
  200.6 1.1 constant_dynamic-slice_fusion.7
  203.8 1.0 pad_maximum_fusion.3
  204.9 2.6 copy.110
  207.4 3.5 select_add_fusion.2
  210.9 1.1 constant_dynamic-update-slice_fusion.2
  213.2 1.1 constant_dynamic-slice_fusion.7
  216.5 1.0 pad_maximum_fusion.3
  217.6 2.6 copy.110
  220.1 3.5 select_add_fusion.2
  223.6 1.1 constant_dynamic-update-slice_fusion.2
  224.7 4.7 copy.88
  229.4 55.3 %reduce-scatter.4.cloned.1.call-done = f32[8,16,2048]{2,1,0:T(8,128)} async-done(((f32[32,16,2048]{2,1,0:T(8,128)}), f32[8,16,2048]{2,1,0:T(8,128)}) %reduce-scatter.4.cloned.1.call-update) | async-done | bytes 1048592 | tf_op jit(solution)/shard_map/reduce_scatter | solution.py:32
  284.8 32.6 %reduce-scatter.6.cloned.1.call-done = f32[2,16,2048]{2,1,0:T(8,128)} async-done(((f32[8,16,2048]{2,1,0:T(8,128)}), f32[2,16,2048]{2,1,0:T(8,128)}) %reduce-scatter.6.cloned.1.call-update) | async-done | bytes 262160 | tf_op jit(solution)/shard_map/reduce_scatter | solution.py:32
  317.5 36.4 %reduce-scatter.8.cloned.1.call-done = f32[1,16,2048]{2,1,0:T(8,128)} async-done(((f32[2,16,2048]{2,1,0:T(8,128)}), f32[1,16,2048]{2,1,0:T(8,128)}) %reduce-scatter.8.cloned.1.call-update) | async-done | bytes 131088 | tf_op jit(solution)/shard_map/reduce_scatter | solution.py:32
  353.9 2.5 broadcast_in_dim.32
  356.4 13.5 %all-to-all-start = ((f32[16,16,2048]{2,1,0:T(8,128)}), f32[16,16,2048]{2,1,0:T(8,128)}, u32[]{:S(2)}, u32[]{:S(2)}) async-start(f32[16,16,2048]{2,1,0:T(8,128)} %broadcast_in_dim.32), calls=%async_computation.3 | async-start | bytes 4194304 | tf_op jit(solution)/shard_map/all_to_all | solution.py:48
  369.9 7.6 %gather_fusion = f32[2048,128]{1,0:T(8,128)} fusion(f32[4096,128]{1,0:T(8,128)S(1)} %bitcast.121, s32[2048]{0:T(1024)S(1)} %broadcast_clamp_fusion), kind=kCustom, calls=%fused_computation | custom fusion | bytes 2105344 | tf_op jit(solution)/shard_map/gather | solution.py:121
  377.4 2.5 reshape.163
  380.0 1.6 multiply_reduce_fusion.1
  381.7 0.7 copy.89
  382.4 5.6 %gather_fusion.1 = bf16[2048,128]{1,0:T(8,128)(2,1)S(1)} fusion(f32[4096,128]{1,0:T(8,128)S(1)} %bitcast.118, s32[2048]{0:T(1024)S(1)} %broadcast_clamp_fusion), kind=kCustom, calls=%fused_computation.1 | custom fusion | bytes 1056768 | tf_op jit(solution)/shard_map/gather | solution.py:165
  388.0 1.0 convert_element_type.46
  389.4 1.2 fusion.15
  390.5 73.0 %all-to-all-done = f32[16,16,2048]{2,1,0:T(8,128)} async-done(((f32[16,16,2048]{2,1,0:T(8,128)}), f32[16,16,2048]{2,1,0:T(8,128)}, u32[]{:S(2)}, u32[]{:S(2)}) %all-to-all-start) | async-done | bytes 2097184 | tf_op jit(solution)/shard_map/all_to_all | solution.py:48
  463.5 1.7 reduce_sum.64
  (118 shorter events, 24.6 us)
Async XLA Ops:
  7.2 24.3 %copy-start.10 = (bf16[128,2048]{1,0:T(8,128)(2,1)S(1)}, bf16[128,2048]{1,0:T(8,128)(2,1)}, u32[]{:S(2)}) copy-start(bf16[128,2048]{1,0:T(8,128)(2,1)} %param.11) | copy-start | bytes 1572868
  7.2 128.2 %all-gather.2.cloned.1.call-start = ((), (), s32[]{:S(2)}) async-start(), calls=%async_computation.4 | async-start | bytes 2162688 | tf_op jit(solution)/shard_map/all_gather | solution.py:23
  8.7 276.1 %reduce-scatter.4.cloned.1.call-start = ((), (), s32[]{:S(2)}) async-start(), calls=%async_computation.5 | async-start | bytes 5242880 | tf_op jit(solution)/shard_map/reduce_scatter | solution.py:32
  12.4 20.1 %copy-start.9 = (bf16[128,2048]{1,0:T(8,128)(2,1)S(1)}, bf16[128,2048]{1,0:T(8,128)(2,1)}, u32[]{:S(2)}) copy-start(bf16[128,2048]{1,0:T(8,128)(2,1)} %param.16) | copy-start | bytes 1572868
  32.7 14.1 %copy-start.5 = (f32[2048,128]{1,0:T(8,128)}, f32[2048,128]{1,0:T(8,128)S(1)}, u32[]{:S(2)}) copy-start(f32[2048,128]{1,0:T(8,128)S(1)} %reshape.170) | copy-start | bytes 3145732
  46.9 1.0 copy-start.7
  145.3 1.6 copy-start.2
  148.3 1.4 copy-start.3
  151.9 1.6 copy-start.2
  154.9 1.4 copy-start.3
  158.5 1.6 copy-start.2
  161.5 1.4 copy-start.3
  165.1 1.6 copy-start.2
  168.0 1.4 copy-start.3
  183.7 1.8 copy-start
  194.7 3.5 copy-start
  207.4 3.5 copy-start
  220.1 3.5 copy-start
  229.4 88.1 %reduce-scatter.6.cloned.1.call-start = ((), (), s32[]{:S(2)}) async-start(), calls=%async_computation.6 | async-start | bytes 1310720 | tf_op jit(solution)/shard_map/reduce_scatter | solution.py:32
  284.8 69.1 %reduce-scatter.8.cloned.1.call-start = ((), (), s32[]{:S(2)}) async-start(), calls=%async_computation.7 | async-start | bytes 393216 | tf_op jit(solution)/shard_map/reduce_scatter | solution.py:32
  356.4 13.5 %copy-start.4 = (f32[8,512,128]{2,1,0:T(8,128)S(1)}, f32[8,512,128]{2,1,0:T(8,128)}, u32[]{:S(2)}) copy-start(f32[8,512,128]{2,1,0:T(8,128)} %get-tuple-element.275) | copy-start | bytes 6291460
  356.4 107.1 %all-to-all-start = ((f32[16,16,2048]{2,1,0:T(8,128)}), f32[16,16,2048]{2,1,0:T(8,128)}, u32[]{:S(2)}, u32[]{:S(2)}) async-start(f32[16,16,2048]{2,1,0:T(8,128)} %broadcast_in_dim.32), calls=%async_computation.3 | async-start | bytes 4194304 | tf_op jit(solution)/shard_map/all_to_all | solution.py:48
  369.9 10.1 %copy-start.6 = (f32[2048,128]{1,0:T(8,128)S(1)}, f32[2048,128]{1,0:T(8,128)}, u32[]{:S(2)}) copy-start(f32[2048,128]{1,0:T(8,128)} %copy-done.5) | copy-start | bytes 3145732
  377.4 4.9 %copy-start.1 = (f32[8,512,128]{2,1,0:T(8,128)S(1)}, f32[8,512,128]{2,1,0:T(8,128)}, u32[]{:S(2)}) copy-start(f32[8,512,128]{2,1,0:T(8,128)} %get-tuple-element.105) | copy-start | bytes 6291460
  388.0 1.4 copy-start.8
Sparse Core Ops, SparseCore 0:
  13.0 122.3 all-gather.1
  229.5 55.2 reduce-scatter.3
  287.8 29.5 reduce-scatter.5
  320.1 33.7 reduce-scatter.7
where the time goes:
time: 474 us; the launch traced here: 472 us
  waiting for transfers between devices  284 us (60%)
  local copies, waits for them, and re-layouts  83.3 us (18%)
  other arithmetic  43.1 us (9%)
  matrix products  28.3 us (6%)
  between operations  14 us (3%)
  starting transfers between devices  13.6 us (3%)
  loops' own time  5.65 us (1%)
    reduce_scatter x3, waiting for transfers between devices, reduced_to_own(): pieces = lax.psum_scatter(pieces, axes[k], scatter_dimension=0, tiled=True)  124 us
    all_gather x1, waiting for transfers between devices, side_by_side(): lax.all_gather(both, axis, axis=dim, tiled=True)  87 us
    all_to_all x1, waiting for transfers between devices, sent_to_all(): lax.all_to_all(jnp.broadcast_to(shard[None], (size, *shard.shape)), axis,...  73 us
    another operation x3, other arithmetic  18.5 us
    dynamic_update_slice x8, local copies, waits for them, and re-layouts, backward_step(): grads = lax.dynamic_update_slice_in_dim(grads, joined, start, 0)  14.5 us
    all_to_all x1, starting transfers between devices, sent_to_all(): lax.all_to_all(jnp.broadcast_to(shard[None], (size, *shard.shape)), axis,...  13.5 us
    dot_general x4, matrix products, backward_step(): jnp.einsum('hgp,phd->hgd', dscore, key_heads, preferred_element_type=jnp....  12.3 us
  transfers between devices with their start and end apart: 5, of which 5 were waited for; matrix products, arithmetic and copies ran while one was open for 13% of the time, Pallas kernels for 0%

commit v1 on v0

v1 whole, which is shorter than its diff:
```python
import functools
import math

import jax
import jax.numpy as jnp
from jax import lax
from jax.experimental import pallas as pl
from jax.experimental.pallas import tpu as pltpu
from jax.sharding import Mesh
from jax.sharding import PartitionSpec as P

HEAD = 128
KV_HEADS = 8
TOPK = 16
CLEN = 1024
ROWS = 128
AXES = ("zl", "core", "x", "zh", "y")
CTX = ("x", "zh", "y")
NT = (((1,), (1,)), ((), ()))
NN = (((1,), (0,)), ((), ()))
SCALE = HEAD ** (-0.5)
LOG2E = math.log2(math.e)
F32 = jnp.float32
BF16 = jnp.bfloat16
MESH = pl.DeviceIdType.MESH
VMEM = pl.BlockSpec(memory_space=pltpu.VMEM)
SMEM = pl.BlockSpec(memory_space=pltpu.SMEM)


def place():
    return tuple(lax.axis_index(a) for a in AXES)


def push(src, dst, send, recv, to):
    copy = pltpu.make_async_remote_copy(
        src_ref=src, dst_ref=dst, send_sem=send, recv_sem=recv, device_id=to, device_id_type=MESH
    )
    copy.start()
    return copy


def landed(ref, send, recv, me):
    pltpu.make_async_remote_copy(
        src_ref=ref, dst_ref=ref, send_sem=send, recv_sem=recv, device_id=me, device_id_type=MESH
    ).wait_recv()


def left(ref, send, recv, me):
    pltpu.make_async_remote_copy(
        src_ref=ref, dst_ref=ref, send_sem=send, recv_sem=recv, device_id=me, device_id_type=MESH
    ).wait_send()


def turn(i, d):
    return lax.rem(i + d, 4)


def half(core):
    return pl.ds(pl.multiple_of(core * 512, 512), 512)


def gather_kernel(kp, vp, kf, vf, ss, rs):
    zl, core, x, zh, y = place()
    me = (zl, core, x, zh, y)
    cs = half(core)
    barrier = pltpu.get_barrier_semaphore()
    edge = jnp.logical_or(zl == 0, zl == 7)
    for d in range(1, 4):
        pl.semaphore_signal(barrier, 1, device_id={"x": turn(x, d)}, device_id_type=MESH)
        pl.semaphore_signal(barrier, 1, device_id={"y": turn(y, d)}, device_id_type=MESH)
    pl.semaphore_signal(barrier, 1, device_id={"core": 1 - core}, device_id_type=MESH)
    source = jnp.where(zl < 4, 7, 0)
    pl.semaphore_signal(barrier, 1, device_id={"zh": 1 - zh, "zl": source}, device_id_type=MESH)
    pl.semaphore_wait(barrier, jnp.where(edge, 11, 7))

    def first(zr):
        ksrc = kp.at[:, cs] if zr == 0 else kf.at[1, x, y, :, cs]
        vsrc = vp.at[:, cs] if zr == 0 else vf.at[1, x, y, :, cs]
        for d in range(1, 4):
            a, b = zr * 12 + d - 1, zr * 12 + 3 + d - 1
            push(ksrc, kf.at[zr, x, y, :, cs], ss.at[a], rs.at[a], {"x": turn(x, d)})
            push(vsrc, vf.at[zr, x, y, :, cs], ss.at[b], rs.at[b], {"y": turn(y, d)})

    def second(zr):
        for d in range(1, 4):
            a = zr * 12 + d - 1
            landed(kf.at[zr, x, y, :, cs], ss.at[a], rs.at[a], me)
        for d in range(1, 4):
            a = zr * 12 + 6 + d - 1
            push(kf.at[zr, :, y, :, cs], kf.at[zr, :, y, :, cs], ss.at[a], rs.at[a], {"y": turn(y, d)})
        for d in range(1, 4):
            b = zr * 12 + 3 + d - 1
            landed(vf.at[zr, x, y, :, cs], ss.at[b], rs.at[b], me)
        for d in range(1, 4):
            b = zr * 12 + 9 + d - 1
            push(vf.at[zr, x, :, :, cs], vf.at[zr, x, :, :, cs], ss.at[b], rs.at[b], {"x": turn(x, d)})

    def third(zr):
        for d in range(1, 4):
            a = zr * 12 + 6 + d - 1
            landed(kf.at[zr, :, y, :, cs], ss.at[a], rs.at[a], me)
        push(kf.at[zr, :, :, :, cs], kf.at[zr, :, :, :, cs], ss.at[32 + zr], rs.at[32 + zr], {"core": 1 - core})
        for d in range(1, 4):
            b = zr * 12 + 9 + d - 1
            landed(vf.at[zr, x, :, :, cs], ss.at[b], rs.at[b], me)
        push(vf.at[zr, :, :, :, cs], vf.at[zr, :, :, :, cs], ss.at[34 + zr], rs.at[34 + zr], {"core": 1 - core})

    first(0)

    @pl.when(edge)
    def _():
        base = jnp.where(zl == 0, 4, 0)
        for t in range(4):
            to = {"zh": 1 - zh, "zl": base + t}
            push(kp.at[:, cs], kf.at[1, x, y, :, cs], ss.at[24 + t], rs.at[24], to)
            push(vp.at[:, cs], vf.at[1, x, y, :, cs], ss.at[28 + t], rs.at[25], to)

    kf[0, x, y, :, cs] = kp[:, cs]
    vf[0, x, y, :, cs] = vp[:, cs]
    second(0)
    landed(kf.at[1, x, y, :, cs], ss.at[24], rs.at[24], me)
    landed(vf.at[1, x, y, :, cs], ss.at[25], rs.at[25], me)
    first(1)
    third(0)
    second(1)
    third(1)
    other = half(1 - core)
    for zr in range(2):
        landed(kf.at[zr, :, :, :, other], ss.at[32 + zr], rs.at[32 + zr], me)
        landed(vf.at[zr, :, :, :, other], ss.at[34 + zr], rs.at[34 + zr], me)
    for zr in range(2):
        for d in range(1, 4):
            left(kf.at[zr, x, y, :, cs], ss.at[zr * 12 + d - 1], rs.at[0], me)
            left(vf.at[zr, x, y, :, cs], ss.at[zr * 12 + 3 + d - 1], rs.at[0], me)
            left(kf.at[zr, :, y, :, cs], ss.at[zr * 12 + 6 + d - 1], rs.at[0], me)
            left(vf.at[zr, x, :, :, cs], ss.at[zr * 12 + 9 + d - 1], rs.at[0], me)
        left(kf.at[zr, :, :, :, cs], ss.at[32 + zr], rs.at[0], me)
        left(vf.at[zr, :, :, :, cs], ss.at[34 + zr], rs.at[0], me)

    @pl.when(edge)
    def _():
        for t in range(8):
            left(kp.at[:, cs], ss.at[24 + t], rs.at[0], me)


def reduce_kernel(gv, gk, out_k, out_v, r0, p0, r1a, r1b, p1a, p1b, r2a, r2b, p2, r3, fin, ss, rs):
    zl, core, x, zh, y = place()
    me = (zl, core, x, zh, y)
    own, other = half(core), half(1 - core)
    parity, turn_z = lax.rem(zl, 2), lax.div(zl, 2)
    grads = (gv, gk)
    barrier = pltpu.get_barrier_semaphore()
    for d in range(1, 4):
        pl.semaphore_signal(barrier, 1, device_id={"x": turn(x, d)}, device_id_type=MESH)
        pl.semaphore_signal(barrier, 1, device_id={"y": turn(y, d)}, device_id_type=MESH)
    for t in range(8):
        pl.semaphore_signal(barrier, 1, device_id={"zh": 1 - zh, "zl": t}, device_id_type=MESH)
        pl.semaphore_signal(barrier, 1, device_id={"core": 1 - core, "zl": t}, device_id_type=MESH)
    for t in range(1, 8):
        pl.semaphore_signal(barrier, 1, device_id={"zl": lax.rem(zl + t, 8)}, device_id_type=MESH)
    pl.semaphore_wait(barrier, 29)

    def send0(u):
        push(grads[u].at[:, :, :, :, other], r0.at[u], ss.at[u], rs.at[u], {"core": 1 - core})

    def sum0(u):
        landed(r0.at[u], ss.at[u], rs.at[u], me)
        for zr in range(2):
            p0[u, zr] = (grads[u][zr, :, :, :, own].astype(F32) + r0[u, zr].astype(F32)).astype(BF16)

    def send1(u):
        for d in range(1, 4):
            a, b = 2 + u * 6 + d - 1, 5 + u * 6 + d - 1
            xp, yp = turn(x, d), turn(y, d)
            push(p0.at[u, :, xp, :, :, 0:256], r1a.at[u, d - 1], ss.at[a], rs.at[a], {"x": xp})
            push(p0.at[u, :, :, yp, :, 256:512], r1b.at[u, d - 1], ss.at[b], rs.at[b], {"y": yp})

    def sum1(u):
        for d in range(3):
            landed(r1a.at[u, d], ss.at[2 + u * 6 + d], rs.at[2 + u * 6 + d], me)
            landed(r1b.at[u, d], ss.at[5 + u * 6 + d], rs.at[5 + u * 6 + d], me)
        a = p0[u, :, x, :, :, 0:256].astype(F32)
        b = p0[u, :, :, y, :, 256:512].astype(F32)
        for d in range(3):
            a = a + r1a[u, d].astype(F32)
            b = b + r1b[u, d].astype(F32)
        p1a[u] = a.astype(BF16)
        p1b[u] = b.astype(BF16)

    def send2(u):
        for d in range(1, 4):
            a, b = 14 + u * 6 + d - 1, 17 + u * 6 + d - 1
            xp, yp = turn(x, d), turn(y, d)
            push(p1a.at[u, :, yp], r2a.at[u, d - 1], ss.at[a], rs.at[a], {"y": yp})
            push(p1b.at[u, :, xp], r2b.at[u, d - 1], ss.at[b], rs.at[b], {"x": xp})

    def sum2(u):
        for d in range(3):
            landed(r2a.at[u, d], ss.at[14 + u * 6 + d], rs.at[14 + u * 6 + d], me)
            landed(r2b.at[u, d], ss.at[17 + u * 6 + d], rs.at[17 + u * 6 + d], me)
        a = p1a[u, :, y].astype(F32)
        b = p1b[u, :, x].astype(F32)
        for d in range(3):
            a = a + r2a[u, d].astype(F32)
            b = b + r2b[u, d].astype(F32)
        for j in range(2):
            p2[u, :, j] = a[:, :, j * 128 : (j + 1) * 128].astype(BF16)
            p2[u, :, 2 + j] = b[:, :, j * 128 : (j + 1) * 128].astype(BF16)

    def send3(u):
        for zr in range(2):
            zt = zh if zr == 0 else 1 - zh
            for j in range(4):
                at = 26 + u * 8 + zr * 4 + j

                def go(zr=zr, zt=zt, j=j, at=at):
                    push(p2.at[u, zr, j], r3.at[zr, zl], ss.at[at], rs.at[26 + zr * 8 + zl], {"zh": zt, "zl": 2 * j + u})

                if zr == 0:
                    pl.when(zl != 2 * j + u)(go)
                else:
                    go()

    def sum3(u):
        @pl.when(parity == u)
        def _():
            for zr in range(2):
                for t in range(8):
                    def get(zr=zr, t=t):
                        landed(r3.at[zr, t], ss.at[26], rs.at[26 + zr * 8 + t], me)

                    if zr == 0:
                        pl.when(zl != t)(get)
                    else:
                        get()
            r3[0, zl] = p2[u, 0, turn_z]
            acc = r3[0, 0].astype(F32)
            for i in range(1, 16):
                acc = acc + r3[i // 8, i % 8].astype(F32)
            fin[u, core, turn_z] = acc.astype(BF16)
            for c in range(2):
                for t in range(8):
                    def go(c=c, t=t):
                        push(
                            fin.at[u, core, turn_z], fin.at[u, core, turn_z], ss.at[42 + c * 8 + t],
                            rs.at[42 + u * 8 + core * 4 + turn_z], {"core": c, "zl": t},
                        )

                    pl.when(jnp.logical_or(core != c, zl != t))(go)

    def finish(u, out):
        for c in range(2):
            for j in range(4):
                @pl.when(jnp.logical_or(core != c, zl != 2 * j + u))
                def _(c=c, j=j):
                    landed(fin.at[u, c, j], ss.at[42], rs.at[42 + u * 8 + c * 4 + j], me)

                out[:, (c * 4 + j) * 128 : (c * 4 + j + 1) * 128] = fin[u, c, j].astype(F32)

    for u in range(2):
        send0(u)
    for u in range(2):
        sum0(u)
        send1(u)
    for u in range(2):
        sum1(u)
        send2(u)
    for u in range(2):
        sum2(u)
        send3(u)
    for u in range(2):
        sum3(u)
    finish(0, out_v)
    finish(1, out_k)
    for u in range(2):
        left(r0.at[u], ss.at[u], rs.at[0], me)
        for d in range(3):
            left(r1a.at[u, d], ss.at[2 + u * 6 + d], rs.at[0], me)
            left(r1b.at[u, d], ss.at[5 + u * 6 + d], rs.at[0], me)
            left(r2a.at[u, d], ss.at[14 + u * 6 + d], rs.at[0], me)
            left(r2b.at[u, d], ss.at[17 + u * 6 + d], rs.at[0], me)
        for zr in range(2):
            for j in range(4):
                def done(u=u, zr=zr, j=j):
                    left(p2.at[u, zr, j], ss.at[26 + u * 8 + zr * 4 + j], rs.at[0], me)

                if zr == 0:
                    pl.when(zl != 2 * j + u)(done)
                else:
                    done()
    for c in range(2):
        for t in range(8):
            @pl.when(jnp.logical_or(core != c, zl != t))
            def _(c=c, t=t):
                left(fin.at[0, 0, 0], ss.at[42 + c * 8 + t], rs.at[0], me)


def compute_kernel(len_ref, eT, gT, q, do, k, v, att, dq, ggT, dk, dv, qx, dx, pf, ds, vt, kt):
    zl, core, x, zh, y = place()
    block = ((zl * 2 + core) * 32) + ((x * 2 + zh) * 4 + y)
    per = CLEN // ROWS
    length = len_ref[lax.div(block, per)]
    token = lax.broadcasted_iota(jnp.int32, (1, ROWS), 1) + lax.rem(block, per) * ROWS
    live = (token < length).astype(F32)
    headT = lax.div(eT[...], 8)
    for p in range(TOPK):
        rows = slice(p * 128, (p + 1) * 128)
        hc = jnp.transpose(jnp.broadcast_to(headT[p : p + 1, :].astype(F32), (128, 128)))
        q32 = q[:, rows].astype(F32)
        d32 = do[:, rows].astype(F32)
        for h in range(KV_HEADS):
            mine = hc == float(h)
            cols = slice(h * 128, (h + 1) * 128)
            qx[rows, cols] = jnp.where(mine, q32, 0.0).astype(BF16)
            dx[rows, cols] = jnp.where(mine, d32, 0.0).astype(BF16)
    lv = jnp.concatenate([live, live], axis=1)
    for kk in range(8):
        rows = pl.ds(kk * 256, 256)
        s = lax.dot_general(k[...], qx[rows, :], NT, preferred_element_type=F32)
        dp = lax.dot_general(v[...], dx[rows, :], NT, preferred_element_type=F32)
        m = jnp.max(s, axis=0, keepdims=True)
        e = jnp.exp2((s - m) * (SCALE * LOG2E))
        inv = 1.0 / jnp.sum(e, axis=0, keepdims=True)
        g = jnp.sum(e * dp, axis=0, keepdims=True) * inv
        gate = jnp.concatenate([gT[2 * kk : 2 * kk + 1, :], gT[2 * kk + 1 : 2 * kk + 2, :]], axis=1)
        w = e * (gate * lv * inv)
        pf[:, rows] = w.astype(BF16)
        ds[:, rows] = (w * (dp - g)).astype(BF16)
        gg = g * lv
        ggT[2 * kk : 2 * kk + 1, :] = gg[:, :128]
        ggT[2 * kk + 1 : 2 * kk + 2, :] = gg[:, 128:]
    for c in range(4):
        cols = pl.ds(c * 256, 256)
        dv[:, cols] = lax.dot_general(pf[...], dx[:, cols], NN, preferred_element_type=F32).astype(BF16)
    for c in range(4):
        cols = pl.ds(c * 256, 256)
        dk[:, cols] = (lax.dot_general(ds[...], qx[:, cols], NN, preferred_element_type=F32) * SCALE).astype(BF16)
    vt[...] = jnp.transpose(v[...])
    kt[...] = jnp.transpose(k[...])
    for src, mat, out, by in ((pf, vt, att, 1.0), (ds, kt, dq, SCALE)):
        for kk in range(8):
            hd = jnp.concatenate([headT[2 * kk : 2 * kk + 1, :], headT[2 * kk + 1 : 2 * kk + 2, :]], axis=1)
            full = lax.dot_general(mat[...], src[:, kk * 256 : (kk + 1) * 256], NN, preferred_element_type=F32)
            acc = full[:128, :]
            for h in range(1, KV_HEADS):
                acc = jnp.where(hd == h, full[h * 128 : (h + 1) * 128, :], acc)
            acc = acc * by
            for j in range(2):
                at = (2 * kk + j) * 128
                out[:, at : at + 128] = jnp.transpose(acc[:, j * 128 : (j + 1) * 128]).astype(BF16)


def local(queries, experts, gate, prefix_keys, prefix_values, d_out, lengths):
    full = jax.ShapeDtypeStruct((2, 4, 4, 16, 1024), BF16)
    kf, vf = pl.pallas_call(
        gather_kernel,
        out_shape=(full, full),
        in_specs=[VMEM] * 2,
        out_specs=(VMEM,) * 2,
        scratch_shapes=[pltpu.SemaphoreType.DMA((36,)), pltpu.SemaphoreType.DMA((36,))],
        compiler_params=pltpu.CompilerParams(collective_id=0, has_side_effects=True, vmem_limit_bytes=16 << 20),
        name="gather",
    )(prefix_keys, prefix_values)
    rows = jax.ShapeDtypeStruct((ROWS, TOPK * HEAD), BF16)
    grad = jax.ShapeDtypeStruct((512, 1024), BF16)
    att, dq, ggT, dk, dv = pl.pallas_call(
        compute_kernel,
        out_shape=(rows, rows, jax.ShapeDtypeStruct((TOPK, ROWS), F32), grad, grad),
        in_specs=[SMEM] + [VMEM] * 6,
        out_specs=(VMEM,) * 5,
        scratch_shapes=[
            pltpu.VMEM((2048, 1024), BF16),
            pltpu.VMEM((2048, 1024), BF16),
            pltpu.VMEM((512, 2048), BF16),
            pltpu.VMEM((512, 2048), BF16),
            pltpu.VMEM((1024, 512), BF16),
            pltpu.VMEM((1024, 512), BF16),
        ],
        compiler_params=pltpu.CompilerParams(vmem_limit_bytes=56 << 20),
        name="attention",
    )(lengths, experts.T, gate.T, queries, d_out, kf.reshape(512, 1024), vf.reshape(512, 1024))
    owned = jax.ShapeDtypeStruct((16, 1024), F32)
    key_grad, value_grad = pl.pallas_call(
        reduce_kernel,
        out_shape=(owned, owned),
        in_specs=[VMEM] * 2,
        out_specs=(VMEM,) * 2,
        scratch_shapes=[
            pltpu.VMEM((2, 2, 4, 4, 16, 512), BF16),
            pltpu.VMEM((2, 2, 4, 4, 16, 512), BF16),
            pltpu.VMEM((2, 3, 2, 4, 16, 256), BF16),
            pltpu.VMEM((2, 3, 2, 4, 16, 256), BF16),
            pltpu.VMEM((2, 2, 4, 16, 256), BF16),
            pltpu.VMEM((2, 2, 4, 16, 256), BF16),
            pltpu.VMEM((2, 3, 2, 16, 256), BF16),
            pltpu.VMEM((2, 3, 2, 16, 256), BF16),
            pltpu.VMEM((2, 2, 4, 16, 128), BF16),
            pltpu.VMEM((2, 8, 16, 128), BF16),
            pltpu.VMEM((2, 2, 4, 16, 128), BF16),
            pltpu.SemaphoreType.DMA((58,)),
            pltpu.SemaphoreType.DMA((58,)),
        ],
        compiler_params=pltpu.CompilerParams(collective_id=1, has_side_effects=True, vmem_limit_bytes=32 << 20),
        name="reduce",
    )(dv.reshape(2, 4, 4, 16, 1024), dk.reshape(2, 4, 4, 16, 1024))
    return att, dq, ggT.T, key_grad, value_grad


def solution(mesh):
    torus = Mesh(mesh.devices.reshape(8, 2, 4, 2, 4), AXES)
    in_specs = (P(AXES, None), P(AXES, None), P(AXES, None), P(CTX, None), P(CTX, None), P(AXES, None), P())
    out_specs = (P(AXES, None), P(AXES, None), P(AXES, None), P(CTX, None), P(CTX, None))
    return jax.shard_map(local, mesh=torus, in_specs=in_specs, out_specs=out_specs, check_vma=False)
```

time: 474 us -> 92.4 us (0.19)
  the two profiles are of different devices: /device:TPU:117 before, /device:TPU:1 now
where the time goes in v1:
time: 92.4 us; the launch traced here: 92.1 us
  Pallas kernels  84.2 us (91%)
  local copies, waits for them, and re-layouts  7.2 us (8%)
    pallas_call x1, Pallas kernels, local(): pl.pallas_call(reduce_kernel, out_shape=(owned, owned), in_specs=[VMEM] *...  34.9 us
    pallas_call x1, Pallas kernels, local(): pl.pallas_call(gather_kernel, out_shape=(full, full), in_specs=[VMEM] * 2...  30.9 us
    pallas_call x1, Pallas kernels, local(): pl.pallas_call(compute_kernel, out_shape=(rows, rows, jax.ShapeDtypeStruc...  18.4 us
    unnamed x14, local copies, waits for them, and re-layouts  7.2 us

profile of v1, /device:TPU:1, one launch (start us, length us, event | category | flops | bytes accessed | tf_op | source)
XLA Modules:
  0.0 92.1 jit_solution(13326714436147155191)
XLA Ops:
  0.6 0.0 copy-start.4
  0.6 0.7 copy-done.4
  1.4 0.0 copy-start.5
  1.4 0.8 copy-done.5
  2.1 30.9 %gather.1 = (bf16[2,4,4,16,1024]{4,3,2,1,0:T(8,128)(2,1)S(1)}, bf16[2,4,4,16,1024]{4,3,2,1,0:T(8,128)(2,1)S(1)}) custom-call(bf16[16,1024]{1,0:T(8,128)(2,1)S(1)} %copy-done.4, bf16[16,1024]{1,0:T(8,128)(2,1)S(1)} %copy-done.5), custom_call_target="tpu_custom_call" | custom-call | tf_op jit(solution)/shard_map/gather/pallas_call | solution.py:355
  33.1 0.0 copy-start.2
  33.1 1.0 %copy-done.2 = bf16[2,4,4,16,1024]{4,3,2,1,0:T(8,128)(2,1)} copy-done((bf16[2,4,4,16,1024]{4,3,2,1,0:T(8,128)(2,1)}, bf16[2,4,4,16,1024]{4,3,2,1,0:T(8,128)(2,1)S(1)}, u32[]{:S(2)}) %copy-start.2) | copy-done | bytes 1048600
  34.0 0.0 copy-start.3
  34.0 1.0 %copy-done.3 = bf16[2,4,4,16,1024]{4,3,2,1,0:T(8,128)(2,1)} copy-done((bf16[2,4,4,16,1024]{4,3,2,1,0:T(8,128)(2,1)}, bf16[2,4,4,16,1024]{4,3,2,1,0:T(8,128)(2,1)S(1)}, u32[]{:S(2)}) %copy-start.3) | copy-done | bytes 1048600
  35.0 18.4 %attention.1 = (bf16[128,2048]{1,0:T(8,128)(2,1)}, bf16[128,2048]{1,0:T(8,128)(2,1)}, f32[16,128]{1,0:T(8,128)}, bf16[512,1024]{1,0:T(8,128)(2,1)}, bf16[512,1024]{1,0:T(8,128)(2,1)}) custom-call(s32[64]{0:T(128)} %len_ref.1, s32[16,128]{1,0:T(8,128)} %bitcast.11, f32[16,128]{1,0:T(8,128)} %bitcast.12, bf16[128,2048]{1,0:T(8,128)(2,1)} %q.1, ...), custom_call_target="tpu_custom_call" | custom-call | tf_op jit(solution)/shard_map/attention/pallas_call | solution.py:366
  53.4 0.0 copy-start
  53.4 1.2 %copy-done = bf16[512,1024]{1,0:T(8,128)(2,1)S(1)} copy-done((bf16[512,1024]{1,0:T(8,128)(2,1)S(1)}, bf16[512,1024]{1,0:T(8,128)(2,1)}, u32[]{:S(2)}) %copy-start) | copy-done | bytes 1048600
  54.6 0.0 copy-start.1
  54.7 1.2 %copy-done.1 = bf16[512,1024]{1,0:T(8,128)(2,1)S(1)} copy-done((bf16[512,1024]{1,0:T(8,128)(2,1)S(1)}, bf16[512,1024]{1,0:T(8,128)(2,1)}, u32[]{:S(2)}) %copy-start.1) | copy-done | bytes 1048600
  55.9 34.9 %reduce.1 = (f32[16,1024]{1,0:T(8,128)S(1)}, f32[16,1024]{1,0:T(8,128)S(1)}) custom-call(bf16[2,4,4,16,1024]{4,3,2,1,0:T(8,128)(2,1)S(1)} %bitcast.8, bf16[2,4,4,16,1024]{4,3,2,1,0:T(8,128)(2,1)S(1)} %bitcast.7), custom_call_target="tpu_custom_call" | custom-call | tf_op jit(solution)/shard_map/reduce/pallas_call | solution.py:383
  90.8 0.6 copy.14
  91.4 0.6 copy.15
Async XLA Ops:
  0.6 0.8 copy-start.4
  1.4 0.8 copy-start.5
  33.1 1.0 %copy-start.2 = (bf16[2,4,4,16,1024]{4,3,2,1,0:T(8,128)(2,1)}, bf16[2,4,4,16,1024]{4,3,2,1,0:T(8,128)(2,1)S(1)}, u32[]{:S(2)}) copy-start(bf16[2,4,4,16,1024]{4,3,2,1,0:T(8,128)(2,1)S(1)} %get-tuple-element.14) | copy-start | bytes 3145732
  34.0 1.0 %copy-start.3 = (bf16[2,4,4,16,1024]{4,3,2,1,0:T(8,128)(2,1)}, bf16[2,4,4,16,1024]{4,3,2,1,0:T(8,128)(2,1)S(1)}, u32[]{:S(2)}) copy-start(bf16[2,4,4,16,1024]{4,3,2,1,0:T(8,128)(2,1)S(1)} %get-tuple-element.15) | copy-start | bytes 3145732
  53.4 1.2 %copy-start = (bf16[512,1024]{1,0:T(8,128)(2,1)S(1)}, bf16[512,1024]{1,0:T(8,128)(2,1)}, u32[]{:S(2)}) copy-start(bf16[512,1024]{1,0:T(8,128)(2,1)} %get-tuple-element.20) | copy-start | bytes 3145732
  54.6 1.2 %copy-start.1 = (bf16[512,1024]{1,0:T(8,128)(2,1)S(1)}, bf16[512,1024]{1,0:T(8,128)(2,1)}, u32[]{:S(2)}) copy-start(bf16[512,1024]{1,0:T(8,128)(2,1)} %get-tuple-element.19) | copy-start | bytes 3145732

commit v2 on v1

v2 whole, which is shorter than its diff:
```python
import functools
import math

import jax
import jax.numpy as jnp
from jax import lax
from jax.experimental import pallas as pl
from jax.experimental.pallas import tpu as pltpu
from jax.sharding import Mesh
from jax.sharding import PartitionSpec as P

HEAD = 128
KV_HEADS = 8
TOPK = 16
CLEN = 1024
ROWS = 128
AXES = ("zl", "core", "x", "zh", "y")
CTX = ("x", "zh", "y")
NT = (((1,), (1,)), ((), ()))
NN = (((1,), (0,)), ((), ()))
SCALE = HEAD ** (-0.5)
LOG2E = math.log2(math.e)
F32 = jnp.float32
BF16 = jnp.bfloat16
MESH = pl.DeviceIdType.MESH
VMEM = pl.BlockSpec(memory_space=pltpu.VMEM)
SMEM = pl.BlockSpec(memory_space=pltpu.SMEM)


def place():
    return tuple(lax.axis_index(a) for a in AXES)


def push(src, dst, send, recv, to):
    copy = pltpu.make_async_remote_copy(
        src_ref=src, dst_ref=dst, send_sem=send, recv_sem=recv, device_id=to, device_id_type=MESH
    )
    copy.start()
    return copy


def landed(ref, send, recv, me):
    pltpu.make_async_remote_copy(
        src_ref=ref, dst_ref=ref, send_sem=send, recv_sem=recv, device_id=me, device_id_type=MESH
    ).wait_recv()


def left(ref, send, recv, me):
    pltpu.make_async_remote_copy(
        src_ref=ref, dst_ref=ref, send_sem=send, recv_sem=recv, device_id=me, device_id_type=MESH
    ).wait_send()


def turn(i, d):
    return lax.rem(i + d, 4)


def half(core):
    return pl.ds(pl.multiple_of(core * 512, 512), 512)


def kernel(
    len_ref, eT_in, gT_in, q_in, d_in, kp, vp,
    att, dq, ggT, out_k, out_v,
    eT, gT, q, do, kf, vf, qx, dx, s0, d0, pf, ds, vt, kt,
    far, near, r0, p0, r1, p1, r2, p2, r3, fin, ls, gs, gr, ss, rs,
):
    zl, core, x, zh, y = place()
    me = (zl, core, x, zh, y)
    cs, other = half(core), half(1 - core)
    parity, turn_z = lax.rem(zl, 2), lax.div(zl, 2)
    edge = jnp.logical_or(zl == 0, zl == 7)

    loads = [
        pltpu.make_async_copy(kp.at[:, cs], kf.at[0, x, y, :, cs], ls.at[0]),
        pltpu.make_async_copy(vp.at[:, cs], vf.at[0, x, y, :, cs], ls.at[1]),
        pltpu.make_async_copy(eT_in, eT, ls.at[2]),
        pltpu.make_async_copy(gT_in, gT, ls.at[3]),
        pltpu.make_async_copy(q_in, q, ls.at[4]),
        pltpu.make_async_copy(d_in, do, ls.at[5]),
    ]
    for c in loads:
        c.start()

    barrier = pltpu.get_barrier_semaphore()
    for d in range(1, 4):
        pl.semaphore_signal(barrier, 1, device_id={"x": turn(x, d)}, device_id_type=MESH)
        pl.semaphore_signal(barrier, 1, device_id={"y": turn(y, d)}, device_id_type=MESH)
    for t in range(8):
        pl.semaphore_signal(barrier, 1, device_id={"zh": 1 - zh, "zl": t}, device_id_type=MESH)
        pl.semaphore_signal(barrier, 1, device_id={"core": 1 - core, "zl": t}, device_id_type=MESH)
    for t in range(1, 8):
        pl.semaphore_signal(barrier, 1, device_id={"zl": lax.rem(zl + t, 8)}, device_id_type=MESH)

    for c in loads[2:]:
        c.wait()
    headT = lax.div(eT[...], 8)
    for p in range(TOPK):
        rows = slice(p * 128, (p + 1) * 128)
        hc = jnp.transpose(jnp.broadcast_to(headT[p : p + 1, :].astype(F32), (128, 128)))
        q32 = q[:, rows].astype(F32)
        d32 = do[:, rows].astype(F32)
        for h in range(KV_HEADS):
            mine = hc == float(h)
            cols = slice(h * 128, (h + 1) * 128)
            qx[rows, cols] = jnp.where(mine, q32, 0.0).astype(BF16)
            dx[rows, cols] = jnp.where(mine, d32, 0.0).astype(BF16)
    for c in loads[:2]:
        c.wait()
    pl.semaphore_wait(barrier, 29)

    def gpush(src, dst, at, to):
        push(src, dst, gs.at[at], gr.at[at], to)

    def glanded(ref, at):
        landed(ref, gs.at[at], gr.at[at], me)

    def first(zr):
        for d in range(1, 4):
            a, b = zr * 12 + d - 1, zr * 12 + 3 + d - 1
            gpush(kf.at[zr, x, y, :, cs], kf.at[zr, x, y, :, cs], a, {"x": turn(x, d)})
            gpush(vf.at[zr, x, y, :, cs], vf.at[zr, x, y, :, cs], b, {"y": turn(y, d)})

    def second(zr):
        for d in range(3):
            glanded(kf.at[zr, x, y, :, cs], zr * 12 + d)
        for d in range(1, 4):
            gpush(kf.at[zr, :, y, :, cs], kf.at[zr, :, y, :, cs], zr * 12 + 6 + d - 1, {"y": turn(y, d)})
        for d in range(3):
            glanded(vf.at[zr, x, y, :, cs], zr * 12 + 3 + d)
        for d in range(1, 4):
            gpush(vf.at[zr, x, :, :, cs], vf.at[zr, x, :, :, cs], zr * 12 + 9 + d - 1, {"x": turn(x, d)})

    def third(zr):
        for d in range(3):
            glanded(kf.at[zr, :, y, :, cs], zr * 12 + 6 + d)
        gpush(kf.at[zr, :, :, :, cs], kf.at[zr, :, :, :, cs], 32 + zr, {"core": 1 - core})
        for d in range(3):
            glanded(vf.at[zr, x, :, :, cs], zr * 12 + 9 + d)
        gpush(vf.at[zr, :, :, :, cs], vf.at[zr, :, :, :, cs], 34 + zr, {"core": 1 - core})

    def swapped(zr):
        glanded(kf.at[zr, :, :, :, other], 32 + zr)
        glanded(vf.at[zr, :, :, :, other], 34 + zr)

    @pl.when(edge)
    def _():
        base = jnp.where(zl == 0, 4, 0)
        for t in range(4):
            to = {"zh": 1 - zh, "zl": base + t}
            push(kf.at[0, x, y, :, cs], kf.at[1, x, y, :, cs], gs.at[24 + t], gr.at[24], to)
            push(vf.at[0, x, y, :, cs], vf.at[1, x, y, :, cs], gs.at[28 + t], gr.at[25], to)

    first(0)
    second(0)
    glanded(kf.at[1, x, y, :, cs], 24)
    glanded(vf.at[1, x, y, :, cs], 25)
    first(1)
    third(0)
    second(1)
    swapped(0)
    k0, v0 = kf[0].reshape(256, 1024), vf[0].reshape(256, 1024)
    for kk in range(8):
        rows = pl.ds(kk * 256, 256)
        s0[:, rows] = lax.dot_general(k0, qx[rows, :], NT, preferred_element_type=F32)
        d0[:, rows] = lax.dot_general(v0, dx[rows, :], NT, preferred_element_type=F32)
    third(1)
    swapped(1)

    block = ((zl * 2 + core) * 32) + ((x * 2 + zh) * 4 + y)
    per = CLEN // ROWS
    length = len_ref[lax.div(block, per)]
    token = lax.broadcasted_iota(jnp.int32, (1, ROWS), 1) + lax.rem(block, per) * ROWS
    live = (token < length).astype(F32)
    lv = jnp.concatenate([live, live], axis=1)
    k1, v1 = kf[1].reshape(256, 1024), vf[1].reshape(256, 1024)
    for kk in range(8):
        rows = pl.ds(kk * 256, 256)
        s = jnp.concatenate(
            [s0[:, rows], lax.dot_general(k1, qx[rows, :], NT, preferred_element_type=F32)], axis=0
        )
        dp = jnp.concatenate(
            [d0[:, rows], lax.dot_general(v1, dx[rows, :], NT, preferred_element_type=F32)], axis=0
        )
        m = jnp.max(s, axis=0, keepdims=True)
        e = jnp.exp2((s - m) * (SCALE * LOG2E))
        inv = 1.0 / jnp.sum(e, axis=0, keepdims=True)
        g = jnp.sum(e * dp, axis=0, keepdims=True) * inv
        gate = jnp.concatenate([gT[2 * kk : 2 * kk + 1, :], gT[2 * kk + 1 : 2 * kk + 2, :]], axis=1)
        w = e * (gate * lv * inv)
        pf[:, rows] = w.astype(BF16)
        ds[:, rows] = (w * (dp - g)).astype(BF16)
        gg = g * lv
        ggT[2 * kk : 2 * kk + 1, :] = gg[:, :128]
        ggT[2 * kk + 1 : 2 * kk + 2, :] = gg[:, 128:]

    def product(u, base, n):
        left_side, right_side = ((pf, dx), (ds, qx))[u]
        cols = pl.ds(pl.multiple_of(base * 512 + n * 256, 256), 256)
        made = lax.dot_general(left_side[...], right_side[:, cols], NN, preferred_element_type=F32)
        if u == 1:
            made = made * SCALE
        return made.reshape(2, 4, 4, 16, 256)

    def send0(u, n):
        far[u, n] = product(u, 1 - core, n).astype(BF16)
        at = u * 2 + n
        push(far.at[u, n], r0.at[u, n], ss.at[at], rs.at[at], {"core": 1 - core})

    def send1(u, n):
        near[...] = product(u, core, n)
        at = u * 2 + n
        landed(r0.at[u, n], ss.at[at], rs.at[at], me)
        p0[u, n] = (near[...] + r0[u, n].astype(F32)).astype(BF16)
        for d in range(1, 4):
            at = 4 + (u * 2 + n) * 3 + d - 1
            if n == 0:
                xp = turn(x, d)
                push(p0.at[u, n, :, xp], r1.at[u, n, d - 1], ss.at[at], rs.at[at], {"x": xp})
            else:
                yp = turn(y, d)
                push(p0.at[u, n, :, :, yp], r1.at[u, n, d - 1], ss.at[at], rs.at[at], {"y": yp})

    def send2(u):
        for n in range(2):
            for d in range(3):
                at = 4 + (u * 2 + n) * 3 + d
                landed(r1.at[u, n, d], ss.at[at], rs.at[at], me)
            own = p0[u, n, :, x] if n == 0 else p0[u, n, :, :, y]
            acc = own.astype(F32)
            for d in range(3):
                acc = acc + r1[u, n, d].astype(F32)
            p1[u, n] = acc.astype(BF16)
            for d in range(1, 4):
                at = 16 + (u * 2 + n) * 3 + d - 1
                if n == 0:
                    yp = turn(y, d)
                    push(p1.at[u, n, :, yp], r2.at[u, n, d - 1], ss.at[at], rs.at[at], {"y": yp})
                else:
                    xp = turn(x, d)
                    push(p1.at[u, n, :, xp], r2.at[u, n, d - 1], ss.at[at], rs.at[at], {"x": xp})

    def send3(u):
        for n in range(2):
            for d in range(3):
                at = 16 + (u * 2 + n) * 3 + d
                landed(r2.at[u, n, d], ss.at[at], rs.at[at], me)
            own = p1[u, n, :, y] if n == 0 else p1[u, n, :, x]
            acc = own.astype(F32)
            for d in range(3):
                acc = acc + r2[u, n, d].astype(F32)
            for j in range(2):
                p2[u, :, 2 * n + j] = acc[:, :, j * 128 : (j + 1) * 128].astype(BF16)
        for zr in range(2):
            zt = zh if zr == 0 else 1 - zh
            for j in range(4):
                at = 28 + u * 8 + zr * 4 + j

                def go(zr=zr, zt=zt, j=j, at=at):
                    push(
                        p2.at[u, zr, j], r3.at[zr, zl], ss.at[at], rs.at[28 + zr * 8 + zl],
                        {"zh": zt, "zl": 2 * j + u},
                    )

                if zr == 0:
                    pl.when(zl != 2 * j + u)(go)
                else:
                    go()

    def send4(u):
        @pl.when(parity == u)
        def _():
            for zr in range(2):
                for t in range(8):
                    def get(zr=zr, t=t):
                        landed(r3.at[zr, t], ss.at[28], rs.at[28 + zr * 8 + t], me)

                    if zr == 0:
                        pl.when(zl != t)(get)
                    else:
                        get()
            r3[0, zl] = p2[u, 0, turn_z]
            acc = r3[0, 0].astype(F32)
            for i in range(1, 16):
                acc = acc + r3[i // 8, i % 8].astype(F32)
            fin[u, core, turn_z] = acc.astype(BF16)
            for c in range(2):
                for t in range(8):
                    def go(c=c, t=t):
                        push(
                            fin.at[u, core, turn_z], fin.at[u, core, turn_z], ss.at[44 + c * 8 + t],
                            rs.at[44 + u * 8 + core * 4 + turn_z], {"core": c, "zl": t},
                        )

                    pl.when(jnp.logical_or(core != c, zl != t))(go)

    def finish(u, out):
        for c in range(2):
            for j in range(4):
                @pl.when(jnp.logical_or(core != c, zl != 2 * j + u))
                def _(c=c, j=j):
                    landed(fin.at[u, c, j], ss.at[44], rs.at[44 + u * 8 + c * 4 + j], me)

                out[:, (c * 4 + j) * 128 : (c * 4 + j + 1) * 128] = fin[u, c, j].astype(F32)

    def rows_out(src, mat, out, by):
        for kk in range(8):
            hd = jnp.concatenate([headT[2 * kk : 2 * kk + 1, :], headT[2 * kk + 1 : 2 * kk + 2, :]], axis=1)
            full = lax.dot_general(mat[...], src[:, kk * 256 : (kk + 1) * 256], NN, preferred_element_type=F32)
            acc = full[:128, :]
            for h in range(1, KV_HEADS):
                acc = jnp.where(hd == h, full[h * 128 : (h + 1) * 128, :], acc)
            acc = acc * by
            for j in range(2):
                at = (2 * kk + j) * 128
                out[:, at : at + 128] = jnp.transpose(acc[:, j * 128 : (j + 1) * 128]).astype(BF16)

    for u in range(2):
        send0(u, 0)
        send0(u, 1)
        send1(u, 0)
        send1(u, 1)
    send2(0)
    send2(1)
    send3(0)
    send3(1)
    vt[...] = jnp.transpose(vf[...].reshape(512, 1024))
    rows_out(pf, vt, att, 1.0)
    send4(0)
    kt[...] = jnp.transpose(kf[...].reshape(512, 1024))
    rows_out(ds, kt, dq, SCALE)
    send4(1)
    finish(0, out_v)
    finish(1, out_k)

    for zr in range(2):
        for d in range(3):
            left(kf.at[zr, x, y, :, cs], gs.at[zr * 12 + d], gr.at[0], me)
            left(vf.at[zr, x, y, :, cs], gs.at[zr * 12 + 3 + d], gr.at[0], me)
            left(kf.at[zr, :, y, :, cs], gs.at[zr * 12 + 6 + d], gr.at[0], me)
            left(vf.at[zr, x, :, :, cs], gs.at[zr * 12 + 9 + d], gr.at[0], me)
        left(kf.at[zr, :, :, :, cs], gs.at[32 + zr], gr.at[0], me)
        left(vf.at[zr, :, :, :, cs], gs.at[34 + zr], gr.at[0], me)

    @pl.when(edge)
    def _():
        for t in range(8):
            left(kf.at[0, x, y, :, cs], gs.at[24 + t], gr.at[0], me)

    for u in range(2):
        for n in range(2):
            left(far.at[u, n], ss.at[u * 2 + n], rs.at[0], me)
            for d in range(3):
                left(r1.at[u, n, d], ss.at[4 + (u * 2 + n) * 3 + d], rs.at[0], me)
                left(r2.at[u, n, d], ss.at[16 + (u * 2 + n) * 3 + d], rs.at[0], me)
        for zr in range(2):
            for j in range(4):
                def done(u=u, zr=zr, j=j):
                    left(p2.at[u, zr, j], ss.at[28 + u * 8 + zr * 4 + j], rs.at[0], me)

                if zr == 0:
                    pl.when(zl != 2 * j + u)(done)
                else:
                    done()
    for c in range(2):
        for t in range(8):
            @pl.when(jnp.logical_or(core != c, zl != t))
            def _(c=c, t=t):
                left(fin.at[0, 0, 0], ss.at[44 + c * 8 + t], rs.at[0], me)


def local(queries, experts, gate, prefix_keys, prefix_values, d_out, lengths):
    rows = jax.ShapeDtypeStruct((ROWS, TOPK * HEAD), BF16)
    owned = jax.ShapeDtypeStruct((16, 1024), F32)
    HBM = pl.BlockSpec(memory_space=pl.ANY)
    full = pltpu.VMEM((2, 4, 4, 16, 1024), BF16)
    att, dq, ggT, key_grad, value_grad = pl.pallas_call(
        kernel,
        out_shape=(rows, rows, jax.ShapeDtypeStruct((TOPK, ROWS), F32), owned, owned),
        in_specs=[SMEM] + [HBM] * 6,
        out_specs=(VMEM,) * 5,
        scratch_shapes=[
            pltpu.VMEM((TOPK, ROWS), jnp.int32),
            pltpu.VMEM((TOPK, ROWS), F32),
            pltpu.VMEM((ROWS, 2048), BF16),
            pltpu.VMEM((ROWS, 2048), BF16),
            full,
            full,
            pltpu.VMEM((2048, 1024), BF16),
            pltpu.VMEM((2048, 1024), BF16),
            pltpu.VMEM((256, 2048), F32),
            pltpu.VMEM((256, 2048), F32),
            pltpu.VMEM((512, 2048), BF16),
            pltpu.VMEM((512, 2048), BF16),
            pltpu.VMEM((1024, 512), BF16),
            pltpu.VMEM((1024, 512), BF16),
            pltpu.VMEM((2, 2, 2, 4, 4, 16, 256), BF16),
            pltpu.VMEM((2, 4, 4, 16, 256), F32),
            pltpu.VMEM((2, 2, 2, 4, 4, 16, 256), BF16),
            pltpu.VMEM((2, 2, 2, 4, 4, 16, 256), BF16),
            pltpu.VMEM((2, 2, 3, 2, 4, 16, 256), BF16),
            pltpu.VMEM((2, 2, 2, 4, 16, 256), BF16),
            pltpu.VMEM((2, 2, 3, 2, 16, 256), BF16),
            pltpu.VMEM((2, 2, 4, 16, 128), BF16),
            pltpu.VMEM((2, 8, 16, 128), BF16),
            pltpu.VMEM((2, 2, 4, 16, 128), BF16),
            pltpu.SemaphoreType.DMA((6,)),
            pltpu.SemaphoreType.DMA((36,)),
            pltpu.SemaphoreType.DMA((36,)),
            pltpu.SemaphoreType.DMA((60,)),
            pltpu.SemaphoreType.DMA((60,)),
        ],
        compiler_params=pltpu.CompilerParams(collective_id=0, has_side_effects=True, vmem_limit_bytes=60 << 20),
        name="prefix",
    )(lengths, experts.T, gate.T, queries, d_out, prefix_keys, prefix_values)
    return att, dq, ggT.T, key_grad, value_grad


def solution(mesh):
    torus = Mesh(mesh.devices.reshape(8, 2, 4, 2, 4), AXES)
    in_specs = (P(AXES, None), P(AXES, None), P(AXES, None), P(CTX, None), P(CTX, None), P(AXES, None), P())
    out_specs = (P(AXES, None), P(AXES, None), P(AXES, None), P(CTX, None), P(CTX, None))
    return jax.shard_map(local, mesh=torus, in_specs=in_specs, out_specs=out_specs, check_vma=False)
```

time: 92.4 us -> 77.4 us (0.84)
  Pallas kernels: 84.2 us -> 71.7 us
  local copies, waits for them, and re-layouts: 7.2 us -> 4.83 us
    pallas_call x3 -> x1, Pallas kernels: 84.2 us -> 71.7 us  [local(): pl.pallas_call(kernel, out_shape=(rows, rows, jax.ShapeDtypeStruct((TOPK,...]
    unnamed x14 -> x13, local copies, waits for them, and re-layouts: 7.2 us -> 4.83 us
where the time goes in v2:
time: 77.4 us; the launch traced here: 77.2 us
  Pallas kernels  71.7 us (93%)
  local copies, waits for them, and re-layouts  4.83 us (6%)
    pallas_call x1, Pallas kernels, local(): pl.pallas_call(kernel, out_shape=(rows, rows, jax.ShapeDtypeStruct((TOPK,...  71.7 us
    unnamed x13, local copies, waits for them, and re-layouts  4.83 us

profile of v2, /device:TPU:1, one launch (start us, length us, event | category | flops | bytes accessed | tf_op | source)
XLA Modules:
  0.0 77.2 jit_solution(13347170558398782927)
XLA Ops:
  0.6 71.7 %prefix.1 = (bf16[128,2048]{1,0:T(8,128)(2,1)}, bf16[128,2048]{1,0:T(8,128)(2,1)}, f32[16,128]{1,0:T(8,128)}, f32[16,1024]{1,0:T(8,128)}, f32[16,1024]{1,0:T(8,128)}) custom-call(s32[64]{0:T(128)} %len_ref.1, s32[16,128]{1,0:T(8,128)} %bitcast.3, f32[16,128]{1,0:T(8,128)} %bitcast.4, bf16[128,2048]{1,0:T(8,128)(2,1)} %q_in.1, bf16[128,2048]{1,0:T(8,128)(2,1)} %d_in.1, ...), custom_call_target="tpu_custom_call" | custom-call | tf_op jit(solution)/shard_map/prefix/pallas_call | solution.py:377
  72.4 0.0 copy-start
  72.4 1.9 %copy.17 = bf16[128,2048]{1,0:T(8,128)(2,1)} copy(bf16[128,2048]{1,0:T(8,128)(2,1)} %get-tuple-element.20) | data formatting | bytes 1048576
  74.3 0.0 copy-done
  74.3 0.0 copy-start.3
  74.3 0.0 copy-start.2
  74.3 0.8 %copy.18 = bf16[128,2048]{1,0:T(8,128)(2,1)} copy(bf16[128,2048]{1,0:T(8,128)(2,1)S(1)} %copy-done) | data formatting | bytes 1048576
  75.1 0.0 copy-done.3
  75.1 0.6 copy.19
  75.7 0.0 copy-done.2
  75.7 0.0 copy-start.1
  75.7 0.6 copy.20
  76.4 0.2 copy-done.1
  76.6 0.6 copy.21
Async XLA Ops:
  72.4 2.0 %copy-start = (bf16[128,2048]{1,0:T(8,128)(2,1)S(1)}, bf16[128,2048]{1,0:T(8,128)(2,1)}, u32[]{:S(2)}) copy-start(bf16[128,2048]{1,0:T(8,128)(2,1)} %get-tuple-element.21) | copy-start | bytes 1572868
  74.3 0.8 %copy-start.3 = (f32[16,128]{1,0:T(8,128)S(1)}, f32[16,128]{1,0:T(8,128)}, u32[]{:S(2)}) copy-start(f32[16,128]{1,0:T(8,128)} %get-tuple-element.12) | copy-start | bytes 24580
  74.3 1.4 %copy-start.2 = (f32[16,1024]{1,0:T(8,128)S(1)}, f32[16,1024]{1,0:T(8,128)}, u32[]{:S(2)}) copy-start(f32[16,1024]{1,0:T(8,128)} %get-tuple-element.23) | copy-start | bytes 196612
  75.7 0.9 %copy-start.1 = (f32[16,1024]{1,0:T(8,128)S(1)}, f32[16,1024]{1,0:T(8,128)}, u32[]{:S(2)}) copy-start(f32[16,1024]{1,0:T(8,128)} %get-tuple-element.24) | copy-start | bytes 196612

commit v3 on v2

--- a/solution.py
+++ b/solution.py
@@ -60,15 +60,15 @@
 
 
 def kernel(
-    len_ref, eT_in, gT_in, q_in, d_in, kp, vp,
+    len_in, eT_in, gT_in, q_in, d_in, kp, vp,
     att, dq, ggT, out_k, out_v,
-    eT, gT, q, do, kf, vf, qx, dx, s0, d0, pf, ds, vt, kt,
-    far, near, r0, p0, r1, p1, r2, p2, r3, fin, ls, gs, gr, ss, rs,
+    len_ref, eT, gT, q, do, kf, vf, qx, dx, s0, d0, pf, ds, vt, kt,
+    far, near, r0, p0, r1, p1, r2, p2, r3, fin, ls, gs, gr, ss, rs, known, both,
 ):
     zl, core, x, zh, y = place()
     me = (zl, core, x, zh, y)
     cs, other = half(core), half(1 - core)
-    parity, turn_z = lax.rem(zl, 2), lax.div(zl, 2)
+    owner, mine_j = jnp.logical_and(zl >= 2, zl < 6), jnp.clip(zl - 2, 0, 3)
     edge = jnp.logical_or(zl == 0, zl == 7)
 
     loads = [
@@ -78,20 +78,69 @@
         pltpu.make_async_copy(gT_in, gT, ls.at[3]),
         pltpu.make_async_copy(q_in, q, ls.at[4]),
         pltpu.make_async_copy(d_in, do, ls.at[5]),
+        pltpu.make_async_copy(len_in, len_ref, ls.at[6]),
     ]
     for c in loads:
         c.start()
+
+    def along_z(d):
+        z = lax.rem(zh * 8 + zl + d, 16)
+        return {"zh": lax.div(z, 8), "zl": lax.rem(z, 8)}
 
     barrier = pltpu.get_barrier_semaphore()
     for d in range(1, 4):
         pl.semaphore_signal(barrier, 1, device_id={"x": turn(x, d)}, device_id_type=MESH)
         pl.semaphore_signal(barrier, 1, device_id={"y": turn(y, d)}, device_id_type=MESH)
-    for t in range(8):
-        pl.semaphore_signal(barrier, 1, device_id={"zh": 1 - zh, "zl": t}, device_id_type=MESH)
-        pl.semaphore_signal(barrier, 1, device_id={"core": 1 - core, "zl": t}, device_id_type=MESH)
-    for t in range(1, 8):
-        pl.semaphore_signal(barrier, 1, device_id={"zl": lax.rem(zl + t, 8)}, device_id_type=MESH)
-
+    pl.semaphore_signal(barrier, 1, device_id={"core": 1 - core}, device_id_type=MESH)
+    for d in (1, 2, 3, 4, 12, 13, 14, 15):
+        pl.semaphore_signal(barrier, 1, device_id=along_z(d), device_id_type=MESH)
+    pl.semaphore_wait(barrier, 15)
+
+    def gpush(src, dst, at, to):
+        push(src, dst, gs.at[at], gr.at[at], to)
+
+    def glanded(ref, at):
+        landed(ref, gs.at[at], gr.at[at], me)
+
+    def first(zr):
+        for d in range(1, 4):
+            a, b = zr * 12 + d - 1, zr * 12 + 3 + d - 1
+            gpush(kp.at[:, cs] if zr == 0 else kf.at[1, x, y, :, cs], kf.at[zr, x, y, :, cs], a, {"x": turn(x, d)})
+            gpush(vp.at[:, cs] if zr == 0 else vf.at[1, x, y, :, cs], vf.at[zr, x, y, :, cs], b, {"y": turn(y, d)})
+
+    def second(zr):
+        for d in range(3):
+            glanded(kf.at[zr, x, y, :, cs], zr * 12 + d)
+        for d in range(1, 4):
+            gpush(kf.at[zr, :, y, :, cs], kf.at[zr, :, y, :, cs], zr * 12 + 6 + d - 1, {"y": turn(y, d)})
+        for d in range(3):
+            glanded(vf.at[zr, x, y, :, cs], zr * 12 + 3 + d)
+        for d in range(1, 4):
+            gpush(vf.at[zr, x, :, :, cs], vf.at[zr, x, :, :, cs], zr * 12 + 9 + d - 1, {"x": turn(x, d)})
+
+    def third(zr):
+        for d in range(3):
+            glanded(kf.at[zr, :, y, :, cs], zr * 12 + 6 + d)
+        gpush(kf.at[zr, :, :, :, cs], kf.at[zr, :, :, :, cs], 32 + zr, {"core": 1 - core})
+        for d in range(3):
+            glanded(vf.at[zr, x, :, :, cs], zr * 12 + 9 + d)
+        gpush(vf.at[zr, :, :, :, cs], vf.at[zr, :, :, :, cs], 34 + zr, {"core": 1 - core})
+
+    def swapped(zr):
+        glanded(kf.at[zr, :, :, :, other], 32 + zr)
+        glanded(vf.at[zr, :, :, :, other], 34 + zr)
+
+    @pl.when(edge)
+    def _():
+        base = jnp.where(zl == 0, 4, 0)
+        for t in range(4):
+            to = {"zh": 1 - zh, "zl": base + t}
+            push(kp.at[:, cs], kf.at[1, x, y, :, cs], gs.at[24 + t], gr.at[24], to)
+            push(vp.at[:, cs], vf.at[1, x, y, :, cs], gs.at[28 + t], gr.at[25], to)
+
+    first(0)
+    for d in (4, 12):
+        pl.semaphore_signal(known, 1, device_id=along_z(d), device_id_type=MESH)
     for c in loads[2:]:
         c.wait()
     headT = lax.div(eT[...], 8)
@@ -107,51 +156,6 @@
             dx[rows, cols] = jnp.where(mine, d32, 0.0).astype(BF16)
     for c in loads[:2]:
         c.wait()
-    pl.semaphore_wait(barrier, 29)
-
-    def gpush(src, dst, at, to):
-        push(src, dst, gs.at[at], gr.at[at], to)
-
-    def glanded(ref, at):
-        landed(ref, gs.at[at], gr.at[at], me)
-
-    def first(zr):
-        for d in range(1, 4):
-            a, b = zr * 12 + d - 1, zr * 12 + 3 + d - 1
-            gpush(kf.at[zr, x, y, :, cs], kf.at[zr, x, y, :, cs], a, {"x": turn(x, d)})
-            gpush(vf.at[zr, x, y, :, cs], vf.at[zr, x, y, :, cs], b, {"y": turn(y, d)})
-
-    def second(zr):
-        for d in range(3):
-            glanded(kf.at[zr, x, y, :, cs], zr * 12 + d)
-        for d in range(1, 4):
-            gpush(kf.at[zr, :, y, :, cs], kf.at[zr, :, y, :, cs], zr * 12 + 6 + d - 1, {"y": turn(y, d)})
-        for d in range(3):
-            glanded(vf.at[zr, x, y, :, cs], zr * 12 + 3 + d)
-        for d in range(1, 4):
-            gpush(vf.at[zr, x, :, :, cs], vf.at[zr, x, :, :, cs], zr * 12 + 9 + d - 1, {"x": turn(x, d)})
-
-    def third(zr):
-        for d in range(3):
-            glanded(kf.at[zr, :, y, :, cs], zr * 12 + 6 + d)
-        gpush(kf.at[zr, :, :, :, cs], kf.at[zr, :, :, :, cs], 32 + zr, {"core": 1 - core})
-        for d in range(3):
-            glanded(vf.at[zr, x, :, :, cs], zr * 12 + 9 + d)
-        gpush(vf.at[zr, :, :, :, cs], vf.at[zr, :, :, :, cs], 34 + zr, {"core": 1 - core})
-
-    def swapped(zr):
-        glanded(kf.at[zr, :, :, :, other], 32 + zr)
-        glanded(vf.at[zr, :, :, :, other], 34 + zr)
-
-    @pl.when(edge)
-    def _():
-        base = jnp.where(zl == 0, 4, 0)
-        for t in range(4):
-            to = {"zh": 1 - zh, "zl": base + t}
-            push(kf.at[0, x, y, :, cs], kf.at[1, x, y, :, cs], gs.at[24 + t], gr.at[24], to)
-            push(vf.at[0, x, y, :, cs], vf.at[1, x, y, :, cs], gs.at[28 + t], gr.at[25], to)
-
-    first(0)
     second(0)
     glanded(kf.at[1, x, y, :, cs], 24)
     glanded(vf.at[1, x, y, :, cs], 25)
@@ -258,38 +262,38 @@
 
                 def go(zr=zr, zt=zt, j=j, at=at):
                     push(
-                        p2.at[u, zr, j], r3.at[zr, zl], ss.at[at], rs.at[28 + zr * 8 + zl],
-                        {"zh": zt, "zl": 2 * j + u},
+                        p2.at[u, zr, j], r3.at[u, zr, zl], ss.at[at], rs.at[28 + u * 16 + zr * 8 + zl],
+                        {"zh": zt, "zl": 2 + j},
                     )
 
                 if zr == 0:
-                    pl.when(zl != 2 * j + u)(go)
+                    pl.when(zl != 2 + j)(go)
                 else:
                     go()
 
     def send4(u):
-        @pl.when(parity == u)
+        @pl.when(owner)
         def _():
             for zr in range(2):
                 for t in range(8):
                     def get(zr=zr, t=t):
-                        landed(r3.at[zr, t], ss.at[28], rs.at[28 + zr * 8 + t], me)
+                        landed(r3.at[u, zr, t], ss.at[28], rs.at[28 + u * 16 + zr * 8 + t], me)
 
                     if zr == 0:
                         pl.when(zl != t)(get)
                     else:
                         get()
-            r3[0, zl] = p2[u, 0, turn_z]
-            acc = r3[0, 0].astype(F32)
+            r3[u, 0, zl] = p2[u, 0, mine_j]
+            acc = r3[u, 0, 0].astype(F32)
             for i in range(1, 16):
-                acc = acc + r3[i // 8, i % 8].astype(F32)
-            fin[u, core, turn_z] = acc.astype(BF16)
+                acc = acc + r3[u, i // 8, i % 8].astype(F32)
+            fin[u, core, mine_j] = acc.astype(BF16)
             for c in range(2):
                 for t in range(8):
                     def go(c=c, t=t):
                         push(
-                            fin.at[u, core, turn_z], fin.at[u, core, turn_z], ss.at[44 + c * 8 + t],
-                            rs.at[44 + u * 8 + core * 4 + turn_z], {"core": c, "zl": t},
+                            fin.at[u, core, mine_j], fin.at[u, core, mine_j], ss.at[44 + u * 16 + c * 8 + t],
+                            rs.at[60 + u * 8 + core * 4 + mine_j], {"core": c, "zl": t},
                         )
 
                     pl.when(jnp.logical_or(core != c, zl != t))(go)
@@ -297,9 +301,9 @@
     def finish(u, out):
         for c in range(2):
             for j in range(4):
-                @pl.when(jnp.logical_or(core != c, zl != 2 * j + u))
+                @pl.when(jnp.logical_or(core != c, zl != 2 + j))
                 def _(c=c, j=j):
-                    landed(fin.at[u, c, j], ss.at[44], rs.at[44 + u * 8 + c * 4 + j], me)
+                    landed(fin.at[u, c, j], ss.at[44], rs.at[60 + u * 8 + c * 4 + j], me)
 
                 out[:, (c * 4 + j) * 128 : (c * 4 + j + 1) * 128] = fin[u, c, j].astype(F32)
 
@@ -322,10 +326,13 @@
         send1(u, 1)
     send2(0)
     send2(1)
+    pl.semaphore_wait(known, 2)
+    pl.semaphore_signal(both, 1, device_id={"core": 1 - core}, device_id_type=MESH)
     send3(0)
     send3(1)
     vt[...] = jnp.transpose(vf[...].reshape(512, 1024))
     rows_out(pf, vt, att, 1.0)
+    pl.semaphore_wait(both, 1)
     send4(0)
     kt[...] = jnp.transpose(kf[...].reshape(512, 1024))
     rows_out(ds, kt, dq, SCALE)
@@ -359,27 +366,44 @@
                     left(p2.at[u, zr, j], ss.at[28 + u * 8 + zr * 4 + j], rs.at[0], me)
 
                 if zr == 0:
-                    pl.when(zl != 2 * j + u)(done)
+                    pl.when(zl != 2 + j)(done)
                 else:
                     done()
-    for c in range(2):
-        for t in range(8):
-            @pl.when(jnp.logical_or(core != c, zl != t))
-            def _(c=c, t=t):
-                left(fin.at[0, 0, 0], ss.at[44 + c * 8 + t], rs.at[0], me)
+    @pl.when(owner)
+    def _():
+        for u in range(2):
+            for c in range(2):
+                for t in range(8):
+                    @pl.when(jnp.logical_or(core != c, zl != t))
+                    def _(u=u, c=c, t=t):
+                        left(fin.at[0, 0, 0], ss.at[44 + u * 16 + c * 8 + t], rs.at[0], me)
+
+
+def copy_kernel(*refs):
+    given, made, held, sem_in, sem_out = refs[:5], refs[5:10], refs[10:15], refs[15], refs[16]
+    ins = [pltpu.make_async_copy(given[i], held[i], sem_in.at[i]) for i in range(5)]
+    outs = [pltpu.make_async_copy(held[i], made[i], sem_out.at[i]) for i in range(5)]
+    for c in ins:
+        c.start()
+    for i in range(5):
+        ins[i].wait()
+        outs[i].start()
+    for c in outs:
+        c.wait()
 
 
 def local(queries, experts, gate, prefix_keys, prefix_values, d_out, lengths):
     rows = jax.ShapeDtypeStruct((ROWS, TOPK * HEAD), BF16)
     owned = jax.ShapeDtypeStruct((16, 1024), F32)
-    HBM = pl.BlockSpec(memory_space=pl.ANY)
+    HBM = pl.BlockSpec(memory_space=pltpu.HBM)
     full = pltpu.VMEM((2, 4, 4, 16, 1024), BF16)
     att, dq, ggT, key_grad, value_grad = pl.pallas_call(
         kernel,
         out_shape=(rows, rows, jax.ShapeDtypeStruct((TOPK, ROWS), F32), owned, owned),
-        in_specs=[SMEM] + [HBM] * 6,
+        in_specs=[HBM] * 7,
         out_specs=(VMEM,) * 5,
         scratch_shapes=[
+            pltpu.SMEM((64,), jnp.int32),
             pltpu.VMEM((TOPK, ROWS), jnp.int32),
             pltpu.VMEM((TOPK, ROWS), F32),
             pltpu.VMEM((ROWS, 2048), BF16),
@@ -402,17 +426,29 @@
             pltpu.VMEM((2, 2, 2, 4, 16, 256), BF16),
             pltpu.VMEM((2, 2, 3, 2, 16, 256), BF16),
             pltpu.VMEM((2, 2, 4, 16, 128), BF16),
-            pltpu.VMEM((2, 8, 16, 128), BF16),
+            pltpu.VMEM((2, 2, 8, 16, 128), BF16),
             pltpu.VMEM((2, 2, 4, 16, 128), BF16),
-            pltpu.SemaphoreType.DMA((6,)),
+            pltpu.SemaphoreType.DMA((7,)),
             pltpu.SemaphoreType.DMA((36,)),
             pltpu.SemaphoreType.DMA((36,)),
-            pltpu.SemaphoreType.DMA((60,)),
-            pltpu.SemaphoreType.DMA((60,)),
+            pltpu.SemaphoreType.DMA((76,)),
+            pltpu.SemaphoreType.DMA((76,)),
+            pltpu.SemaphoreType.REGULAR,
+            pltpu.SemaphoreType.REGULAR,
         ],
         compiler_params=pltpu.CompilerParams(collective_id=0, has_side_effects=True, vmem_limit_bytes=60 << 20),
         name="prefix",
     )(lengths, experts.T, gate.T, queries, d_out, prefix_keys, prefix_values)
+    made = (att, dq, ggT, key_grad, value_grad)
+    att, dq, ggT, key_grad, value_grad = pl.pallas_call(
+        copy_kernel,
+        out_shape=tuple(jax.ShapeDtypeStruct(a.shape, a.dtype) for a in made),
+        in_specs=[HBM] * 5,
+        out_specs=(HBM,) * 5,
+        scratch_shapes=[pltpu.VMEM(a.shape, a.dtype) for a in made] + [pltpu.SemaphoreType.DMA((5,))] * 2,
+        compiler_params=pltpu.CompilerParams(vmem_limit_bytes=60 << 20),
+        name="results",
+    )(*made)
     return att, dq, ggT.T, key_grad, value_grad
 
 

time: 77.4 us -> 72.4 us (0.935)
  local copies, waits for them, and re-layouts: 4.83 us -> 0 us
    unnamed x13 -> x0, local copies, waits for them, and re-layouts: 4.83 us -> none
    pallas_call x1, Pallas kernels: 71.7 us -> 69.3 us  [local(): pl.pallas_call(kernel, out_shape=(rows, rows, jax.ShapeDtypeStruct((TOPK,...]
    pallas_call x0 -> x1, Pallas kernels: none -> 2.13 us  [local(): pl.pallas_call(copy_kernel, out_shape=tuple((jax.ShapeDtypeStruct(a.shape...]
where the time goes in v3:
time: 72.4 us; the launch traced here: 72.3 us
  Pallas kernels  71.5 us (99%)
  between operations  0.8 us (1%)
    pallas_call x1, Pallas kernels, local(): pl.pallas_call(kernel, out_shape=(rows, rows, jax.ShapeDtypeStruct((TOPK,...  69.3 us
    pallas_call x1, Pallas kernels, local(): pl.pallas_call(copy_kernel, out_shape=tuple((jax.ShapeDtypeStruct(a.shape...  2.13 us

profile of v3, /device:TPU:1, one launch (start us, length us, event | category | flops | bytes accessed | tf_op | source)
XLA Modules:
  0.0 72.3 jit_solution(937865491969014732)
XLA Ops:
  0.6 69.3 %prefix.1 = (bf16[128,2048]{1,0:T(8,128)(2,1)}, bf16[128,2048]{1,0:T(8,128)(2,1)}, f32[16,128]{1,0:T(8,128)}, f32[16,1024]{1,0:T(8,128)}, f32[16,1024]{1,0:T(8,128)}) custom-call(s32[64]{0:T(128)} %len_in.1, s32[16,128]{1,0:T(8,128)} %bitcast.3, f32[16,128]{1,0:T(8,128)} %bitcast.4, bf16[128,2048]{1,0:T(8,128)(2,1)} %q_in.1, bf16[128,2048]{1,0:T(8,128)(2,1)} %d_in.1, ...), custom_call_target="tpu_custom_call" | custom-call | tf_op jit(solution)/shard_map/prefix/pallas_call | solution.py:400
  70.0 2.1 %results.1 = (bf16[128,2048]{1,0:T(8,128)(2,1)}, bf16[128,2048]{1,0:T(8,128)(2,1)}, f32[16,128]{1,0:T(8,128)}, f32[16,1024]{1,0:T(8,128)}, f32[16,1024]{1,0:T(8,128)}) custom-call(bf16[128,2048]{1,0:T(8,128)(2,1)} %get-tuple-element.15.refs_0_, bf16[128,2048]{1,0:T(8,128)(2,1)} %get-tuple-element.16.refs_1_, f32[16,128]{1,0:T(8,128)} %get-tuple-element.17.refs_2_, ...), custom_call_target="tpu_custom_call" | custom-call | tf_op jit(solution)/shard_map/results/pallas_call | solution.py:443

commit v4 on v3

--- a/solution.py
+++ b/solution.py
@@ -102,43 +102,51 @@
     def glanded(ref, at):
         landed(ref, gs.at[at], gr.at[at], me)
 
-    def first(zr):
+    whole, given = (kf, vf), (kp, vp)
+    ca = pl.ds(pl.multiple_of(core * 512, 256), 256)
+    cb = pl.ds(pl.multiple_of(core * 512 + 256, 256), 256)
+
+    def first(m, zr):
+        at, ref = (m * 2 + zr) * 13, whole[m]
         for d in range(1, 4):
-            a, b = zr * 12 + d - 1, zr * 12 + 3 + d - 1
-            gpush(kp.at[:, cs] if zr == 0 else kf.at[1, x, y, :, cs], kf.at[zr, x, y, :, cs], a, {"x": turn(x, d)})
-            gpush(vp.at[:, cs] if zr == 0 else vf.at[1, x, y, :, cs], vf.at[zr, x, y, :, cs], b, {"y": turn(y, d)})
-
-    def second(zr):
+            for n, cols, to in ((0, ca, {"x": turn(x, d)}), (3, cb, {"y": turn(y, d)})):
+                src = given[m].at[:, cols] if zr == 0 else ref.at[1, x, y, :, cols]
+                gpush(src, ref.at[zr, x, y, :, cols], at + n + d - 1, to)
+
+    def second(m, zr):
+        at, ref = (m * 2 + zr) * 13, whole[m]
         for d in range(3):
-            glanded(kf.at[zr, x, y, :, cs], zr * 12 + d)
+            glanded(ref.at[zr, x, y, :, ca], at + d)
         for d in range(1, 4):
-            gpush(kf.at[zr, :, y, :, cs], kf.at[zr, :, y, :, cs], zr * 12 + 6 + d - 1, {"y": turn(y, d)})
+            gpush(ref.at[zr, :, y, :, ca], ref.at[zr, :, y, :, ca], at + 6 + d - 1, {"y": turn(y, d)})
         for d in range(3):
-            glanded(vf.at[zr, x, y, :, cs], zr * 12 + 3 + d)
+            glanded(ref.at[zr, x, y, :, cb], at + 3 + d)
         for d in range(1, 4):
-            gpush(vf.at[zr, x, :, :, cs], vf.at[zr, x, :, :, cs], zr * 12 + 9 + d - 1, {"x": turn(x, d)})
-
-    def third(zr):
+            gpush(ref.at[zr, x, :, :, cb], ref.at[zr, x, :, :, cb], at + 9 + d - 1, {"x": turn(x, d)})
+
+    def third(m, zr):
+        at, ref = (m * 2 + zr) * 13, whole[m]
         for d in range(3):
-            glanded(kf.at[zr, :, y, :, cs], zr * 12 + 6 + d)
-        gpush(kf.at[zr, :, :, :, cs], kf.at[zr, :, :, :, cs], 32 + zr, {"core": 1 - core})
-        for d in range(3):
-            glanded(vf.at[zr, x, :, :, cs], zr * 12 + 9 + d)
-        gpush(vf.at[zr, :, :, :, cs], vf.at[zr, :, :, :, cs], 34 + zr, {"core": 1 - core})
-
-    def swapped(zr):
-        glanded(kf.at[zr, :, :, :, other], 32 + zr)
-        glanded(vf.at[zr, :, :, :, other], 34 + zr)
-
-    @pl.when(edge)
-    def _():
-        base = jnp.where(zl == 0, 4, 0)
-        for t in range(4):
-            to = {"zh": 1 - zh, "zl": base + t}
-            push(kp.at[:, cs], kf.at[1, x, y, :, cs], gs.at[24 + t], gr.at[24], to)
-            push(vp.at[:, cs], vf.at[1, x, y, :, cs], gs.at[28 + t], gr.at[25], to)
-
-    first(0)
+            glanded(ref.at[zr, :, y, :, ca], at + 6 + d)
+            glanded(ref.at[zr, x, :, :, cb], at + 9 + d)
+        gpush(ref.at[zr, :, :, :, cs], ref.at[zr, :, :, :, cs], at + 12, {"core": 1 - core})
+
+    def swapped(m, zr):
+        glanded(whole[m].at[zr, :, :, :, other], (m * 2 + zr) * 13 + 12)
+
+    def across(m):
+        @pl.when(edge)
+        def _():
+            base = jnp.where(zl == 0, 4, 0)
+            for t in range(4):
+                to = {"zh": 1 - zh, "zl": base + t}
+                push(given[m].at[:, cs], whole[m].at[1, x, y, :, cs], gs.at[54 + m * 4 + t], gr.at[52 + m], to)
+
+    def crossed(m):
+        glanded(whole[m].at[1, x, y, :, cs], 52 + m)
+
+    across(0)
+    first(0, 0)
     for d in (4, 12):
         pl.semaphore_signal(known, 1, device_id=along_z(d), device_id_type=MESH)
     for c in loads[2:]:
@@ -156,20 +164,30 @@
             dx[rows, cols] = jnp.where(mine, d32, 0.0).astype(BF16)
     for c in loads[:2]:
         c.wait()
-    second(0)
-    glanded(kf.at[1, x, y, :, cs], 24)
-    glanded(vf.at[1, x, y, :, cs], 25)
-    first(1)
-    third(0)
-    second(1)
-    swapped(0)
-    k0, v0 = kf[0].reshape(256, 1024), vf[0].reshape(256, 1024)
+    second(0, 0)
+    across(1)
+    first(1, 0)
+    crossed(0)
+    first(0, 1)
+    third(0, 0)
+    second(1, 0)
+    second(0, 1)
+    crossed(1)
+    first(1, 1)
+    swapped(0, 0)
+    k0 = kf[0].reshape(256, 1024)
     for kk in range(8):
         rows = pl.ds(kk * 256, 256)
         s0[:, rows] = lax.dot_general(k0, qx[rows, :], NT, preferred_element_type=F32)
+    third(1, 0)
+    third(0, 1)
+    second(1, 1)
+    swapped(1, 0)
+    v0 = vf[0].reshape(256, 1024)
+    for kk in range(8):
+        rows = pl.ds(kk * 256, 256)
         d0[:, rows] = lax.dot_general(v0, dx[rows, :], NT, preferred_element_type=F32)
-    third(1)
-    swapped(1)
+    swapped(0, 1)
 
     block = ((zl * 2 + core) * 32) + ((x * 2 + zh) * 4 + y)
     per = CLEN // ROWS
@@ -177,26 +195,20 @@
     token = lax.broadcasted_iota(jnp.int32, (1, ROWS), 1) + lax.rem(block, per) * ROWS
     live = (token < length).astype(F32)
     lv = jnp.concatenate([live, live], axis=1)
-    k1, v1 = kf[1].reshape(256, 1024), vf[1].reshape(256, 1024)
+    k1 = kf[1].reshape(256, 1024)
+
+    def gates(kk):
+        return jnp.concatenate([gT[2 * kk : 2 * kk + 1, :], gT[2 * kk + 1 : 2 * kk + 2, :]], axis=1)
+
     for kk in range(8):
         rows = pl.ds(kk * 256, 256)
         s = jnp.concatenate(
             [s0[:, rows], lax.dot_general(k1, qx[rows, :], NT, preferred_element_type=F32)], axis=0
         )
-        dp = jnp.concatenate(
-            [d0[:, rows], lax.dot_general(v1, dx[rows, :], NT, preferred_element_type=F32)], axis=0
-        )
         m = jnp.max(s, axis=0, keepdims=True)
         e = jnp.exp2((s - m) * (SCALE * LOG2E))
         inv = 1.0 / jnp.sum(e, axis=0, keepdims=True)
-        g = jnp.sum(e * dp, axis=0, keepdims=True) * inv
-        gate = jnp.concatenate([gT[2 * kk : 2 * kk + 1, :], gT[2 * kk + 1 : 2 * kk + 2, :]], axis=1)
-        w = e * (gate * lv * inv)
-        pf[:, rows] = w.astype(BF16)
-        ds[:, rows] = (w * (dp - g)).astype(BF16)
-        gg = g * lv
-        ggT[2 * kk : 2 * kk + 1, :] = gg[:, :128]
-        ggT[2 * kk + 1 : 2 * kk + 2, :] = gg[:, 128:]
+        pf[:, rows] = (e * (gates(kk) * lv * inv)).astype(BF16)
 
     def product(u, base, n):
         left_side, right_side = ((pf, dx), (ds, qx))[u]
@@ -319,11 +331,27 @@
                 at = (2 * kk + j) * 128
                 out[:, at : at + 128] = jnp.transpose(acc[:, j * 128 : (j + 1) * 128]).astype(BF16)
 
-    for u in range(2):
-        send0(u, 0)
-        send0(u, 1)
-        send1(u, 0)
-        send1(u, 1)
+    third(1, 1)
+    send0(0, 0)
+    send0(0, 1)
+    send1(0, 0)
+    send1(0, 1)
+    swapped(1, 1)
+    v1 = vf[1].reshape(256, 1024)
+    for kk in range(8):
+        rows = pl.ds(kk * 256, 256)
+        dp = jnp.concatenate(
+            [d0[:, rows], lax.dot_general(v1, dx[rows, :], NT, preferred_element_type=F32)], axis=0
+        )
+        w = pf[:, rows].astype(F32)
+        g = jnp.sum(w * dp, axis=0, keepdims=True) / gates(kk)
+        ds[:, rows] = (w * (dp - g)).astype(BF16)
+        ggT[2 * kk : 2 * kk + 1, :] = g[:, :128]
+        ggT[2 * kk + 1 : 2 * kk + 2, :] = g[:, 128:]
+    send0(1, 0)
+    send0(1, 1)
+    send1(1, 0)
+    send1(1, 1)
     send2(0)
     send2(1)
     pl.semaphore_wait(known, 2)
@@ -340,19 +368,20 @@
     finish(0, out_v)
     finish(1, out_k)
 
-    for zr in range(2):
-        for d in range(3):
-            left(kf.at[zr, x, y, :, cs], gs.at[zr * 12 + d], gr.at[0], me)
-            left(vf.at[zr, x, y, :, cs], gs.at[zr * 12 + 3 + d], gr.at[0], me)
-            left(kf.at[zr, :, y, :, cs], gs.at[zr * 12 + 6 + d], gr.at[0], me)
-            left(vf.at[zr, x, :, :, cs], gs.at[zr * 12 + 9 + d], gr.at[0], me)
-        left(kf.at[zr, :, :, :, cs], gs.at[32 + zr], gr.at[0], me)
-        left(vf.at[zr, :, :, :, cs], gs.at[34 + zr], gr.at[0], me)
+    for m in range(2):
+        for zr in range(2):
+            at, ref = (m * 2 + zr) * 13, whole[m]
+            for d in range(3):
+                left(ref.at[zr, x, y, :, ca], gs.at[at + d], gr.at[0], me)
+                left(ref.at[zr, x, y, :, cb], gs.at[at + 3 + d], gr.at[0], me)
+                left(ref.at[zr, :, y, :, ca], gs.at[at + 6 + d], gr.at[0], me)
+                left(ref.at[zr, x, :, :, cb], gs.at[at + 9 + d], gr.at[0], me)
+            left(ref.at[zr, :, :, :, cs], gs.at[at + 12], gr.at[0], me)
 
     @pl.when(edge)
     def _():
         for t in range(8):
-            left(kf.at[0, x, y, :, cs], gs.at[24 + t], gr.at[0], me)
+            left(kf.at[0, x, y, :, cs], gs.at[54 + t], gr.at[0], me)
 
     for u in range(2):
         for n in range(2):
@@ -429,8 +458,8 @@
             pltpu.VMEM((2, 2, 8, 16, 128), BF16),
             pltpu.VMEM((2, 2, 4, 16, 128), BF16),
             pltpu.SemaphoreType.DMA((7,)),
-            pltpu.SemaphoreType.DMA((36,)),
-            pltpu.SemaphoreType.DMA((36,)),
+            pltpu.SemaphoreType.DMA((62,)),
+            pltpu.SemaphoreType.DMA((62,)),
             pltpu.SemaphoreType.DMA((76,)),
             pltpu.SemaphoreType.DMA((76,)),
             pltpu.SemaphoreType.REGULAR,

time: 72.4 us -> 73.2 us (1.011)
    pallas_call x1, Pallas kernels: 69.3 us -> 70.1 us  [local(): pl.pallas_call(kernel, out_shape=(rows, rows, jax.ShapeDtypeStruct((TOPK,...]
where the time goes in v4:
time: 73.2 us; the launch traced here: 73 us
  Pallas kernels  72.2 us (99%)
  between operations  0.8 us (1%)
    pallas_call x1, Pallas kernels, local(): pl.pallas_call(kernel, out_shape=(rows, rows, jax.ShapeDtypeStruct((TOPK,...  70.1 us
    pallas_call x1, Pallas kernels, local(): pl.pallas_call(copy_kernel, out_shape=tuple((jax.ShapeDtypeStruct(a.shape...  2.13 us

profile of v4, /device:TPU:1, one launch (start us, length us, event | category | flops | bytes accessed | tf_op | source)
XLA Modules:
  0.0 73.0 jit_solution(1745870456593786277)
XLA Ops:
  0.6 70.1 %prefix.1 = (bf16[128,2048]{1,0:T(8,128)(2,1)}, bf16[128,2048]{1,0:T(8,128)(2,1)}, f32[16,128]{1,0:T(8,128)}, f32[16,1024]{1,0:T(8,128)}, f32[16,1024]{1,0:T(8,128)}) custom-call(s32[64]{0:T(128)} %len_in.1, s32[16,128]{1,0:T(8,128)} %bitcast.3, f32[16,128]{1,0:T(8,128)} %bitcast.4, bf16[128,2048]{1,0:T(8,128)(2,1)} %q_in.1, bf16[128,2048]{1,0:T(8,128)(2,1)} %d_in.1, ...), custom_call_target="tpu_custom_call" | custom-call | tf_op jit(solution)/shard_map/prefix/pallas_call | solution.py:429
  70.7 2.1 %results.1 = (bf16[128,2048]{1,0:T(8,128)(2,1)}, bf16[128,2048]{1,0:T(8,128)(2,1)}, f32[16,128]{1,0:T(8,128)}, f32[16,1024]{1,0:T(8,128)}, f32[16,1024]{1,0:T(8,128)}) custom-call(bf16[128,2048]{1,0:T(8,128)(2,1)} %get-tuple-element.15.refs_0_, bf16[128,2048]{1,0:T(8,128)(2,1)} %get-tuple-element.16.refs_1_, f32[16,128]{1,0:T(8,128)} %get-tuple-element.17.refs_2_, ...), custom_call_target="tpu_custom_call" | custom-call | tf_op jit(solution)/shard_map/results/pallas_call | solution.py:472

commit v5 on v3

--- a/solution.py
+++ b/solution.py
@@ -88,11 +88,11 @@
         return {"zh": lax.div(z, 8), "zl": lax.rem(z, 8)}
 
     barrier = pltpu.get_barrier_semaphore()
-    for d in range(1, 4):
+    for d in (2, 1, 3):
         pl.semaphore_signal(barrier, 1, device_id={"x": turn(x, d)}, device_id_type=MESH)
         pl.semaphore_signal(barrier, 1, device_id={"y": turn(y, d)}, device_id_type=MESH)
     pl.semaphore_signal(barrier, 1, device_id={"core": 1 - core}, device_id_type=MESH)
-    for d in (1, 2, 3, 4, 12, 13, 14, 15):
+    for d in (4, 12, 3, 13, 2, 14, 1, 15):
         pl.semaphore_signal(barrier, 1, device_id=along_z(d), device_id_type=MESH)
     pl.semaphore_wait(barrier, 15)
 
@@ -103,7 +103,7 @@
         landed(ref, gs.at[at], gr.at[at], me)
 
     def first(zr):
-        for d in range(1, 4):
+        for d in (2, 1, 3):
             a, b = zr * 12 + d - 1, zr * 12 + 3 + d - 1
             gpush(kp.at[:, cs] if zr == 0 else kf.at[1, x, y, :, cs], kf.at[zr, x, y, :, cs], a, {"x": turn(x, d)})
             gpush(vp.at[:, cs] if zr == 0 else vf.at[1, x, y, :, cs], vf.at[zr, x, y, :, cs], b, {"y": turn(y, d)})
@@ -111,11 +111,11 @@
     def second(zr):
         for d in range(3):
             glanded(kf.at[zr, x, y, :, cs], zr * 12 + d)
-        for d in range(1, 4):
+        for d in (2, 1, 3):
             gpush(kf.at[zr, :, y, :, cs], kf.at[zr, :, y, :, cs], zr * 12 + 6 + d - 1, {"y": turn(y, d)})
         for d in range(3):
             glanded(vf.at[zr, x, y, :, cs], zr * 12 + 3 + d)
-        for d in range(1, 4):
+        for d in (2, 1, 3):
             gpush(vf.at[zr, x, :, :, cs], vf.at[zr, x, :, :, cs], zr * 12 + 9 + d - 1, {"x": turn(x, d)})
 
     def third(zr):
@@ -132,9 +132,8 @@
 
     @pl.when(edge)
     def _():
-        base = jnp.where(zl == 0, 4, 0)
         for t in range(4):
-            to = {"zh": 1 - zh, "zl": base + t}
+            to = {"zh": 1 - zh, "zl": jnp.where(zl == 0, 4 + t, 3 - t)}
             push(kp.at[:, cs], kf.at[1, x, y, :, cs], gs.at[24 + t], gr.at[24], to)
             push(vp.at[:, cs], vf.at[1, x, y, :, cs], gs.at[28 + t], gr.at[25], to)
 
@@ -216,7 +215,7 @@
         at = u * 2 + n
         landed(r0.at[u, n], ss.at[at], rs.at[at], me)
         p0[u, n] = (near[...] + r0[u, n].astype(F32)).astype(BF16)
-        for d in range(1, 4):
+        for d in (2, 1, 3):
             at = 4 + (u * 2 + n) * 3 + d - 1
             if n == 0:
                 xp = turn(x, d)
@@ -235,7 +234,7 @@
             for d in range(3):
                 acc = acc + r1[u, n, d].astype(F32)
             p1[u, n] = acc.astype(BF16)
-            for d in range(1, 4):
+            for d in (2, 1, 3):
                 at = 16 + (u * 2 + n) * 3 + d - 1
                 if n == 0:
                     yp = turn(y, d)
@@ -255,7 +254,7 @@
                 acc = acc + r2[u, n, d].astype(F32)
             for j in range(2):
                 p2[u, :, 2 * n + j] = acc[:, :, j * 128 : (j + 1) * 128].astype(BF16)
-        for zr in range(2):
+        for zr in (1, 0):
             zt = zh if zr == 0 else 1 - zh
             for j in range(4):
                 at = 28 + u * 8 + zr * 4 + j
@@ -288,8 +287,8 @@
             for i in range(1, 16):
                 acc = acc + r3[u, i // 8, i % 8].astype(F32)
             fin[u, core, mine_j] = acc.astype(BF16)
-            for c in range(2):
-                for t in range(8):
+            for t in (7, 0, 6, 1, 5, 2, 4, 3):
+                for c in range(2):
                     def go(c=c, t=t):
                         push(
                             fin.at[u, core, mine_j], fin.at[u, core, mine_j], ss.at[44 + u * 16 + c * 8 + t],
@@ -319,11 +318,14 @@
                 at = (2 * kk + j) * 128
                 out[:, at : at + 128] = jnp.transpose(acc[:, j * 128 : (j + 1) * 128]).astype(BF16)
 
-    for u in range(2):
-        send0(u, 0)
-        send0(u, 1)
-        send1(u, 0)
-        send1(u, 1)
+    send0(0, 0)
+    send0(0, 1)
+    send0(1, 0)
+    send1(0, 0)
+    send1(0, 1)
+    send0(1, 1)
+    send1(1, 0)
+    send1(1, 1)
     send2(0)
     send2(1)
     pl.semaphore_wait(known, 2)
@@ -331,15 +333,9 @@
     send3(0)
     send3(1)
     vt[...] = jnp.transpose(vf[...].reshape(512, 1024))
-    rows_out(pf, vt, att, 1.0)
-    pl.semaphore_wait(both, 1)
-    send4(0)
-    kt[...] = jnp.transpose(kf[...].reshape(512, 1024))
-    rows_out(ds, kt, dq, SCALE)
-    send4(1)
-    finish(0, out_v)
-    finish(1, out_k)
-
+    rows_out(pf, vt, q, 1.0)
+    att_out = pltpu.make_async_copy(q, att, ls.at[0])
+    att_out.start()
     for zr in range(2):
         for d in range(3):
             left(kf.at[zr, x, y, :, cs], gs.at[zr * 12 + d], gr.at[0], me)
@@ -360,6 +356,14 @@
             for d in range(3):
                 left(r1.at[u, n, d], ss.at[4 + (u * 2 + n) * 3 + d], rs.at[0], me)
                 left(r2.at[u, n, d], ss.at[16 + (u * 2 + n) * 3 + d], rs.at[0], me)
+    pl.semaphore_wait(both, 1)
+    send4(0)
+    kt[...] = jnp.transpose(kf[...].reshape(512, 1024))
+    rows_out(ds, kt, do, SCALE)
+    dq_out = pltpu.make_async_copy(do, dq, ls.at[1])
+    dq_out.start()
+    send4(1)
+    for u in range(2):
         for zr in range(2):
             for j in range(4):
                 def done(u=u, zr=zr, j=j):
@@ -369,6 +373,11 @@
                     pl.when(zl != 2 + j)(done)
                 else:
                     done()
+    finish(0, out_v)
+    finish(1, out_k)
+    att_out.wait()
+    dq_out.wait()
+
     @pl.when(owner)
     def _():
         for u in range(2):
@@ -401,7 +410,7 @@
         kernel,
         out_shape=(rows, rows, jax.ShapeDtypeStruct((TOPK, ROWS), F32), owned, owned),
         in_specs=[HBM] * 7,
-        out_specs=(VMEM,) * 5,
+        out_specs=(HBM, HBM, VMEM, VMEM, VMEM),
         scratch_shapes=[
             pltpu.SMEM((64,), jnp.int32),
             pltpu.VMEM((TOPK, ROWS), jnp.int32),

time: 72.4 us -> 70.8 us (0.978)
  Pallas kernels: 71.5 us -> 69.8 us
    pallas_call x1, Pallas kernels: 69.3 us -> 67.7 us  [local(): pl.pallas_call(kernel, out_shape=(rows, rows, jax.ShapeDtypeStruct((TOPK,...]
where the time goes in v5:
time: 70.8 us; the launch traced here: 70.6 us
  Pallas kernels  69.8 us (99%)
  between operations  0.8 us (1%)
    pallas_call x1, Pallas kernels, local(): pl.pallas_call(kernel, out_shape=(rows, rows, jax.ShapeDtypeStruct((TOPK,...  67.7 us
    pallas_call x1, Pallas kernels, local(): pl.pallas_call(copy_kernel, out_shape=tuple((jax.ShapeDtypeStruct(a.shape...  2.13 us

profile of v5, /device:TPU:1, one launch (start us, length us, event | category | flops | bytes accessed | tf_op | source)
XLA Modules:
  0.0 70.6 jit_solution(9373392315538832452)
XLA Ops:
  0.6 67.7 %prefix.1 = (bf16[128,2048]{1,0:T(8,128)(2,1)}, bf16[128,2048]{1,0:T(8,128)(2,1)}, f32[16,128]{1,0:T(8,128)}, f32[16,1024]{1,0:T(8,128)}, f32[16,1024]{1,0:T(8,128)}) custom-call(s32[64]{0:T(128)} %len_in.1, s32[16,128]{1,0:T(8,128)} %bitcast.3, f32[16,128]{1,0:T(8,128)} %bitcast.4, bf16[128,2048]{1,0:T(8,128)(2,1)} %q_in.1, bf16[128,2048]{1,0:T(8,128)(2,1)} %d_in.1, ...), custom_call_target="tpu_custom_call" | custom-call | tf_op jit(solution)/shard_map/prefix/pallas_call | solution.py:409
  68.3 2.1 %results.1 = (bf16[128,2048]{1,0:T(8,128)(2,1)}, bf16[128,2048]{1,0:T(8,128)(2,1)}, f32[16,128]{1,0:T(8,128)}, f32[16,1024]{1,0:T(8,128)}, f32[16,1024]{1,0:T(8,128)}) custom-call(bf16[128,2048]{1,0:T(8,128)(2,1)} %get-tuple-element.15.refs_0_, bf16[128,2048]{1,0:T(8,128)(2,1)} %get-tuple-element.16.refs_1_, f32[16,128]{1,0:T(8,128)} %get-tuple-element.17.refs_2_, ...), custom_call_target="tpu_custom_call" | custom-call | tf_op jit(solution)/shard_map/results/pallas_call | solution.py:452

commit v6 on v5

--- a/solution.py
+++ b/solution.py
@@ -219,16 +219,14 @@
             at = 4 + (u * 2 + n) * 3 + d - 1
             if n == 0:
                 xp = turn(x, d)
-                push(p0.at[u, n, :, xp], r1.at[u, n, d - 1], ss.at[at], rs.at[at], {"x": xp})
+                push(p0.at[u, n, :, xp], r1.at[u, n, d - 1], ss.at[at], rs.at[4 + u * 2 + n], {"x": xp})
             else:
                 yp = turn(y, d)
-                push(p0.at[u, n, :, :, yp], r1.at[u, n, d - 1], ss.at[at], rs.at[at], {"y": yp})
+                push(p0.at[u, n, :, :, yp], r1.at[u, n, d - 1], ss.at[at], rs.at[4 + u * 2 + n], {"y": yp})
 
     def send2(u):
         for n in range(2):
-            for d in range(3):
-                at = 4 + (u * 2 + n) * 3 + d
-                landed(r1.at[u, n, d], ss.at[at], rs.at[at], me)
+            landed(r1.at[u, n], ss.at[0], rs.at[4 + u * 2 + n], me)
             own = p0[u, n, :, x] if n == 0 else p0[u, n, :, :, y]
             acc = own.astype(F32)
             for d in range(3):
@@ -238,16 +236,14 @@
                 at = 16 + (u * 2 + n) * 3 + d - 1
                 if n == 0:
                     yp = turn(y, d)
-                    push(p1.at[u, n, :, yp], r2.at[u, n, d - 1], ss.at[at], rs.at[at], {"y": yp})
+                    push(p1.at[u, n, :, yp], r2.at[u, n, d - 1], ss.at[at], rs.at[8 + u * 2 + n], {"y": yp})
                 else:
                     xp = turn(x, d)
-                    push(p1.at[u, n, :, xp], r2.at[u, n, d - 1], ss.at[at], rs.at[at], {"x": xp})
+                    push(p1.at[u, n, :, xp], r2.at[u, n, d - 1], ss.at[at], rs.at[8 + u * 2 + n], {"x": xp})
 
     def send3(u):
         for n in range(2):
-            for d in range(3):
-                at = 16 + (u * 2 + n) * 3 + d
-                landed(r2.at[u, n, d], ss.at[at], rs.at[at], me)
+            landed(r2.at[u, n], ss.at[0], rs.at[8 + u * 2 + n], me)
             own = p1[u, n, :, y] if n == 0 else p1[u, n, :, x]
             acc = own.astype(F32)
             for d in range(3):
@@ -260,51 +256,47 @@
                 at = 28 + u * 8 + zr * 4 + j
 
                 def go(zr=zr, zt=zt, j=j, at=at):
-                    push(
-                        p2.at[u, zr, j], r3.at[u, zr, zl], ss.at[at], rs.at[28 + u * 16 + zr * 8 + zl],
-                        {"zh": zt, "zl": 2 + j},
-                    )
+                    there = rs.at[28 + u * 16 + zl] if zr == 0 else rs.at[36 + u * 16]
+                    push(p2.at[u, zr, j], r3.at[u, zr, zl], ss.at[at], there, {"zh": zt, "zl": 2 + j})
 
                 if zr == 0:
                     pl.when(zl != 2 + j)(go)
                 else:
                     go()
 
-    def send4(u):
+    def send4():
         @pl.when(owner)
         def _():
-            for zr in range(2):
+            for u in range(2):
                 for t in range(8):
-                    def get(zr=zr, t=t):
-                        landed(r3.at[u, zr, t], ss.at[28], rs.at[28 + u * 16 + zr * 8 + t], me)
-
-                    if zr == 0:
-                        pl.when(zl != t)(get)
-                    else:
-                        get()
-            r3[u, 0, zl] = p2[u, 0, mine_j]
-            acc = r3[u, 0, 0].astype(F32)
-            for i in range(1, 16):
-                acc = acc + r3[u, i // 8, i % 8].astype(F32)
-            fin[u, core, mine_j] = acc.astype(BF16)
+                    @pl.when(zl != t)
+                    def _(u=u, t=t):
+                        landed(r3.at[u, 0, t], ss.at[0], rs.at[28 + u * 16 + t], me)
+
+                landed(r3.at[u, 1], ss.at[0], rs.at[36 + u * 16], me)
+                r3[u, 0, zl] = p2[u, 0, mine_j]
+                acc = r3[u, 0, 0].astype(F32)
+                for i in range(1, 16):
+                    acc = acc + r3[u, i // 8, i % 8].astype(F32)
+                fin[core, mine_j, u] = acc.astype(BF16)
+            tile = fin.at[core, mine_j]
             for t in (7, 0, 6, 1, 5, 2, 4, 3):
                 for c in range(2):
                     def go(c=c, t=t):
-                        push(
-                            fin.at[u, core, mine_j], fin.at[u, core, mine_j], ss.at[44 + u * 16 + c * 8 + t],
-                            rs.at[60 + u * 8 + core * 4 + mine_j], {"core": c, "zl": t},
-                        )
+                        push(tile, tile, ss.at[44 + c * 8 + t], rs.at[60 + core * 4 + mine_j], {"core": c, "zl": t})
 
                     pl.when(jnp.logical_or(core != c, zl != t))(go)
 
-    def finish(u, out):
-        for c in range(2):
-            for j in range(4):
+    def finish():
+        for j in (1, 2, 0, 3):
+            for c in range(2):
                 @pl.when(jnp.logical_or(core != c, zl != 2 + j))
                 def _(c=c, j=j):
-                    landed(fin.at[u, c, j], ss.at[44], rs.at[60 + u * 8 + c * 4 + j], me)
-
-                out[:, (c * 4 + j) * 128 : (c * 4 + j + 1) * 128] = fin[u, c, j].astype(F32)
+                    landed(fin.at[c, j], ss.at[0], rs.at[60 + c * 4 + j], me)
+
+                cols = slice((c * 4 + j) * 128, (c * 4 + j + 1) * 128)
+                out_v[:, cols] = fin[c, j, 0].astype(F32)
+                out_k[:, cols] = fin[c, j, 1].astype(F32)
 
     def rows_out(src, mat, out, by):
         for kk in range(8):
@@ -336,6 +328,10 @@
     rows_out(pf, vt, q, 1.0)
     att_out = pltpu.make_async_copy(q, att, ls.at[0])
     att_out.start()
+    kt[...] = jnp.transpose(kf[...].reshape(512, 1024))
+    rows_out(ds, kt, do, SCALE)
+    dq_out = pltpu.make_async_copy(do, dq, ls.at[1])
+    dq_out.start()
     for zr in range(2):
         for d in range(3):
             left(kf.at[zr, x, y, :, cs], gs.at[zr * 12 + d], gr.at[0], me)
@@ -357,12 +353,7 @@
                 left(r1.at[u, n, d], ss.at[4 + (u * 2 + n) * 3 + d], rs.at[0], me)
                 left(r2.at[u, n, d], ss.at[16 + (u * 2 + n) * 3 + d], rs.at[0], me)
     pl.semaphore_wait(both, 1)
-    send4(0)
-    kt[...] = jnp.transpose(kf[...].reshape(512, 1024))
-    rows_out(ds, kt, do, SCALE)
-    dq_out = pltpu.make_async_copy(do, dq, ls.at[1])
-    dq_out.start()
-    send4(1)
+    send4()
     for u in range(2):
         for zr in range(2):
             for j in range(4):
@@ -373,19 +364,17 @@
                     pl.when(zl != 2 + j)(done)
                 else:
                     done()
-    finish(0, out_v)
-    finish(1, out_k)
+    finish()
     att_out.wait()
     dq_out.wait()
 
     @pl.when(owner)
     def _():
-        for u in range(2):
-            for c in range(2):
-                for t in range(8):
-                    @pl.when(jnp.logical_or(core != c, zl != t))
-                    def _(u=u, c=c, t=t):
-                        left(fin.at[0, 0, 0], ss.at[44 + u * 16 + c * 8 + t], rs.at[0], me)
+        for c in range(2):
+            for t in range(8):
+                @pl.when(jnp.logical_or(core != c, zl != t))
+                def _(c=c, t=t):
+                    left(fin.at[0, 0], ss.at[44 + c * 8 + t], rs.at[0], me)
 
 
 def copy_kernel(*refs):
@@ -436,7 +425,7 @@
             pltpu.VMEM((2, 2, 3, 2, 16, 256), BF16),
             pltpu.VMEM((2, 2, 4, 16, 128), BF16),
             pltpu.VMEM((2, 2, 8, 16, 128), BF16),
-            pltpu.VMEM((2, 2, 4, 16, 128), BF16),
+            pltpu.VMEM((2, 4, 2, 16, 128), BF16),
             pltpu.SemaphoreType.DMA((7,)),
             pltpu.SemaphoreType.DMA((36,)),
             pltpu.SemaphoreType.DMA((36,)),

time: 70.8 us -> 70.7 us (level)
  no operation moved by 1% of the time
where the time goes in v6:
time: 70.7 us; the launch traced here: 70.6 us
  Pallas kernels  69.8 us (99%)
  between operations  0.8 us (1%)
    pallas_call x1, Pallas kernels, local(): pl.pallas_call(kernel, out_shape=(rows, rows, jax.ShapeDtypeStruct((TOPK,...  67.7 us
    pallas_call x1, Pallas kernels, local(): pl.pallas_call(copy_kernel, out_shape=tuple((jax.ShapeDtypeStruct(a.shape...  2.13 us

profile of v6, /device:TPU:1, one launch (start us, length us, event | category | flops | bytes accessed | tf_op | source)
XLA Modules:
  0.0 70.6 jit_solution(6395993102873041892)
XLA Ops:
  0.6 67.7 %prefix.1 = (bf16[128,2048]{1,0:T(8,128)(2,1)}, bf16[128,2048]{1,0:T(8,128)(2,1)}, f32[16,128]{1,0:T(8,128)}, f32[16,1024]{1,0:T(8,128)}, f32[16,1024]{1,0:T(8,128)}) custom-call(s32[64]{0:T(128)} %len_in.1, s32[16,128]{1,0:T(8,128)} %bitcast.3, f32[16,128]{1,0:T(8,128)} %bitcast.4, bf16[128,2048]{1,0:T(8,128)(2,1)} %q_in.1, bf16[128,2048]{1,0:T(8,128)(2,1)} %d_in.1, ...), custom_call_target="tpu_custom_call" | custom-call | tf_op jit(solution)/shard_map/prefix/pallas_call | solution.py:398
  68.3 2.1 %results.1 = (bf16[128,2048]{1,0:T(8,128)(2,1)}, bf16[128,2048]{1,0:T(8,128)(2,1)}, f32[16,128]{1,0:T(8,128)}, f32[16,1024]{1,0:T(8,128)}, f32[16,1024]{1,0:T(8,128)}) custom-call(bf16[128,2048]{1,0:T(8,128)(2,1)} %get-tuple-element.15.refs_0_, bf16[128,2048]{1,0:T(8,128)(2,1)} %get-tuple-element.16.refs_1_, f32[16,128]{1,0:T(8,128)} %get-tuple-element.17.refs_2_, ...), custom_call_target="tpu_custom_call" | custom-call | tf_op jit(solution)/shard_map/results/pallas_call | solution.py:441
